TPU v7x, 512 devices: a whole 4x4x16 slice. The times are simulated.
512 devices in a mesh: tok: 128 (over z, x, core), hd: 4 (over y).
Axes of the slice: x: 4, y: 4, z: 16, core: 2. Of those that a mesh axis runs over, the one named last changes fastest.
Arguments:
- query: bfloat16 [16384, 8192], P('tok', 'hd'), may hold values from -6 to 6
- keys: bfloat16 [16384, 1024], P(('tok', 'hd')), may hold values from -6 to 6
- values: bfloat16 [16384, 1024], P(('tok', 'hd')), may hold values from -6 to 6
- grad_out: bfloat16 [16384, 8192], P('tok', 'hd'), may hold values from -6 to 6
- delta: float32 [16384, 64], P('tok', 'hd'), may hold values from -24 to 24
- segments: int32 [16384], replicated, may hold values from 0 to 127, never falling along the last dimension, each value on 1 to 512 neighbouring positions
Outputs:
- grad_query: bfloat16 [16384, 8192], P('tok', 'hd')
- grad_key: bfloat16 [16384, 1024], P(('tok', 'hd'))
- grad_value: bfloat16 [16384, 1024], P(('tok', 'hd'))
Inputs may be any that keep to these rules, and one draw needn't show every extreme that they name: `segments`: ids never fall along the tokens; each document holds 1 to 512 tokens and one holds exactly 512.
All inputs are finite; a program needn't handle non-finite values.
Results may differ from a plain program's by a relative error of at most 0.0049.
Values may be sent and summed in bfloat16 or wider, within the bound.
A program may use at most 64 MiB of HBM per device.

v0:
```python
import math

import jax
import jax.numpy as jnp
from jax import lax
from jax.sharding import PartitionSpec as P

WIN = 4


NEG_FILL = -1e30


def passed_along(block, axis, distance):
    devices = range(lax.axis_size(axis))
    route = [(i - distance, i) for i in devices if i - distance in devices]
    return lax.ppermute(block, axis, route)


def group_scores(query_group, key_group, allowed, scale_factor):
    raw_scores = (
        jnp.einsum("qrd,kd->rqk", query_group, key_group, preferred_element_type=jnp.float32)
        * scale_factor
    )
    return jnp.where(allowed[None], raw_scores, NEG_FILL)


def group_stats(query_group, key_group, allowed, scale_factor):
    scores = group_scores(query_group, key_group, allowed, scale_factor)
    row_top = jnp.max(scores, axis=-1)
    row_sum = jnp.sum(jnp.where(allowed[None], jnp.exp(scores - row_top[..., None]), 0.0), axis=-1)
    return (row_top, row_sum)


def group_grads(
    query_group,
    grad_group,
    delta_group,
    key_group,
    value_group,
    allowed,
    row_top,
    row_sum,
    scale_factor,
):
    scores = group_scores(query_group, key_group, allowed, scale_factor)
    weights = jnp.where(
        allowed[None], jnp.exp(scores - row_top[..., None]) / row_sum[..., None], 0.0
    )
    weights_low = weights.astype(jnp.bfloat16)
    grad_weights = jnp.einsum(
        "qrd,kd->rqk", grad_group, value_group, preferred_element_type=jnp.float32
    )
    grad_scores = (weights * (grad_weights - delta_group[..., None])).astype(jnp.bfloat16)
    grad_query = (
        jnp.einsum("rqk,kd->qrd", grad_scores, key_group, preferred_element_type=jnp.float32)
        * scale_factor
    )
    grad_key = (
        jnp.einsum("rqk,qrd->kd", grad_scores, query_group, preferred_element_type=jnp.float32)
        * scale_factor
    )
    grad_value = jnp.einsum(
        "rqk,qrd->kd", weights_low, grad_group, preferred_element_type=jnp.float32
    )
    return (grad_query, grad_key, grad_value)


def on_device(query, keys, values, grad_out, delta, segments):
    tok_rows = query.shape[0]
    heads_dev = delta.shape[1]
    width = query.shape[1] // heads_dev
    scale_factor = 1.0 / math.sqrt(width)
    all_keys, all_values = (
        lax.all_gather(keys, "hd", axis=0, tiled=True),
        lax.all_gather(values, "hd", axis=0, tiled=True),
    )
    own_span = all_keys.shape[1] // lax.axis_size("hd")
    col_start = lax.axis_index("hd") * own_span
    own_keys = lax.dynamic_slice_in_dim(all_keys, col_start, own_span, 1)
    own_values = lax.dynamic_slice_in_dim(all_values, col_start, own_span, 1)
    groups = own_keys.shape[1] // width
    repeat = heads_dev // groups
    own_pair = jnp.stack([own_keys, own_values])
    near_pairs = [own_pair]
    for distance in range(1, WIN + 1):
        near_pairs.append(passed_along(own_pair, "tok", distance))
    window_pairs = jnp.concatenate(near_pairs[::-1], axis=1)
    window_keys = window_pairs[0]
    window_values = window_pairs[1]
    lead_rows = WIN * tok_rows
    span_rows = lead_rows + tok_rows
    row_start = lax.axis_index("tok") * tok_rows
    padded_seg = jnp.concatenate([jnp.full((lead_rows,), -1, jnp.int32), segments])
    key_seg = lax.dynamic_slice_in_dim(padded_seg, row_start, span_rows)
    query_seg = lax.dynamic_slice_in_dim(segments, row_start, tok_rows)
    allowed = (key_seg[None, :] == query_seg[:, None]) & (
        jnp.arange(span_rows)[None, :] <= jnp.arange(tok_rows)[:, None] + lead_rows
    )
    query_heads = query.reshape(tok_rows, groups, repeat, width)
    grad_heads = grad_out.reshape(tok_rows, groups, repeat, width)
    delta_heads = delta.reshape(tok_rows, groups, repeat)
    query_parts = []
    key_parts = []
    value_parts = []
    for group in range(groups):
        query_group = query_heads[:, group]
        grad_group = grad_heads[:, group]
        delta_group = delta_heads[:, group].T
        key_group = window_keys[:, group * width : (group + 1) * width]
        value_group = window_values[:, group * width : (group + 1) * width]
        row_top, row_sum = group_stats(query_group, key_group, allowed, scale_factor)
        grad_query, grad_key, grad_value = group_grads(
            query_group,
            grad_group,
            delta_group,
            key_group,
            value_group,
            allowed,
            row_top,
            row_sum,
            scale_factor,
        )
        key_parts.append(grad_key.reshape(WIN + 1, tok_rows, width))
        value_parts.append(grad_value.reshape(WIN + 1, tok_rows, width))
        query_parts.append(grad_query)
    grad_query_out = (
        jnp.stack(query_parts, axis=1).reshape(tok_rows, heads_dev * width).astype(jnp.bfloat16)
    )
    window_grads = jnp.stack(
        [jnp.concatenate(key_parts, axis=2), jnp.concatenate(value_parts, axis=2)], axis=1
    )
    summed = window_grads[WIN]
    for distance in range(1, WIN + 1):
        summed = summed + passed_along(window_grads[WIN - distance], "tok", -distance)
    grad_key_out, grad_value_out = (
        lax.all_to_all(
            summed[0].astype(jnp.bfloat16), "hd", split_axis=0, concat_axis=1, tiled=True
        ),
        lax.all_to_all(
            summed[1].astype(jnp.bfloat16), "hd", split_axis=0, concat_axis=1, tiled=True
        ),
    )
    return (grad_query_out, grad_key_out, grad_value_out)


def solution(mesh):
    return jax.shard_map(
        on_device,
        mesh=mesh,
        in_specs=(
            P("tok", "hd"),
            P(("tok", "hd"), None),
            P(("tok", "hd"), None),
            P("tok", "hd"),
            P("tok", "hd"),
            P(),
        ),
        out_specs=(P("tok", "hd"), P(("tok", "hd"), None), P(("tok", "hd"), None)),
        check_vma=False,
    )
```

profile of v0, /device:TPU:103, one launch (start us, length us, event | category | flops | bytes accessed | tf_op | source)
XLA Modules:
  0.0 112.0 jit_solution(8405951165687189019)
XLA Ops:
  0.6 10.8 %all_gather.7 = bf16[128,1024]{1,0:T(8,128)(2,1)S(1)} all-gather(bf16[32,1024]{1,0:T(8,128)(2,1)} %param.8), channel_id=1, replica_groups=mesh['tok'=128,'hd'=4] {'hd'}, dimensions={0}, use_global_device_ids=true | all-gather | bytes 327680 | tf_op jit(solution)/shard_map/all_gather | solution.py:76
  11.4 9.6 %all_gather.6 = bf16[128,1024]{1,0:T(8,128)(2,1)S(1)} all-gather(bf16[32,1024]{1,0:T(8,128)(2,1)} %param.7), channel_id=1, replica_groups=mesh['tok'=128,'hd'=4] {'hd'}, dimensions={0}, use_global_device_ids=true | all-gather | bytes 327680 | tf_op jit(solution)/shard_map/all_gather | solution.py:75
  21.0 5.6 %collective-permute-start = (bf16[2,128,256]{2,1,0:T(8,128)(2,1)S(1)}, bf16[2,128,256]{2,1,0:T(8,128)(2,1)S(1)}, u32[]{:S(2)}, u32[]{:S(2)}) collective-permute-start(bf16[2,128,256]{2,1,0:T(8,128)(2,1)S(1)} %pad_maximum_fusion.2), channel_id=1, source_target_pairs={{0,16},{4,20},{8,24},{12,28},{16,32},{20,36},{24,40},{28,44},{32,4... | collective-permute-start | bytes 393224 | tf_op jit(solution)/shard_map/ppermute | solution.py:17
  26.6 9.8 %collective-permute-start.1 = (bf16[2,128,256]{2,1,0:T(8,128)(2,1)S(1)}, bf16[2,128,256]{2,1,0:T(8,128)(2,1)S(1)}, u32[]{:S(2)}, u32[]{:S(2)}) collective-permute-start(bf16[2,128,256]{2,1,0:T(8,128)(2,1)S(1)} %pad_maximum_fusion.2), channel_id=1, source_target_pairs={{0,12},{4,16},{8,20},{12,24},{16,28},{20,32},{24,36},{28,40},{32,4... | collective-permute-start | bytes 393224 | tf_op jit(solution)/shard_map/ppermute | solution.py:17
  36.5 3.5 %collective-permute-start.2 = (bf16[2,128,256]{2,1,0:T(8,128)(2,1)S(1)}, bf16[2,128,256]{2,1,0:T(8,128)(2,1)S(1)}, u32[]{:S(2)}, u32[]{:S(2)}) collective-permute-start(bf16[2,128,256]{2,1,0:T(8,128)(2,1)S(1)} %pad_maximum_fusion.2), channel_id=1, source_target_pairs={{0,8},{4,12},{8,16},{12,20},{16,24},{20,28},{24,32},{28,36},{32,40... | collective-permute-start | bytes 393224 | tf_op jit(solution)/shard_map/ppermute | solution.py:17
  40.0 1.9 %collective-permute-start.3 = (bf16[2,128,256]{2,1,0:T(8,128)(2,1)S(1)}, bf16[2,128,256]{2,1,0:T(8,128)(2,1)S(1)}, u32[]{:S(2)}, u32[]{:S(2)}) collective-permute-start(bf16[2,128,256]{2,1,0:T(8,128)(2,1)S(1)} %pad_maximum_fusion.2), channel_id=1, source_target_pairs={{0,4},{4,8},{8,12},{12,16},{16,20},{20,24},{24,28},{28,32},{32,36}... | collective-permute-start | bytes 393224 | tf_op jit(solution)/shard_map/ppermute | solution.py:17
  41.9 0.8 dynamic_slice.15
  42.7 0.8 pad_dynamic-slice_fusion
  43.5 0.2 fusion.12
  43.6 0.8 fusion.13
  44.4 1.3 %slice_bitcast_fusion.19 = (f32[8,128]{1,0:T(8,128)}, f32[8,128]{1,0:T(8,128)}) fusion(f32[128,2,8]{0,2,1:T(8,128)} %bitcast.204), kind=kLoop, calls=%fused_computation.86 | loop fusion | bytes 16384 | tf_op jit(solution)/shard_map/transpose | solution.py:109
  45.7 1.3 %copy.49 = bf16[128,2048]{0,1:T(8,128)(2,1)S(1)} copy(bf16[128,2048]{1,0:T(8,128)(2,1)} %param.6) | data formatting | bytes 1048576 | tf_op args[0]
  47.0 0.0 copy-done.8
  47.0 1.0 copy.51
  48.0 0.0 collective-permute-done
  48.0 0.0 collective-permute-done.1
  48.1 0.0 collective-permute-done.2
  48.1 0.0 collective-permute-done.3
  48.2 0.5 fusion.4
  48.7 0.0 copy-start.11
  48.7 0.6 copy-done.11
  49.3 1.8 %select_reduce_fusion.1 = (f32[8,128]{1,0:T(8,128)}, f32[8,128]{1,0:T(8,128)S(1)}, f32[640,128,8]{1,0,2:T(8,128)S(1)}) fusion(f32[640,128,8]{1,0,2:T(8,128)S(1)} %get-tuple-element.27, f32[8,128]{1,0:T(8,128)S(1)} %get-tuple-element.26, pred[128,640]{0,1:T(8,128)(4,1)S(1)} %fusion.12, bf16[128,2,8,128]{0,3,2,1:T(8,128)(2,1)S(1)} %bitcast.187, ...), kind=kOutput, calls=%fused_computation.12 | convolution fusion | flops 173012992 | bytes 5763072 | tf_op jit(solution)/shard_map/qrd,kd->rqk/dot_general | solution.py:22
  51.1 0.6 select_reduce_fusion
  51.8 0.7 copy-done.5
  52.5 0.0 copy-done.14
  52.5 1.0 fusion.1
  53.5 0.0 copy-done
  53.5 0.0 copy-done.12
  53.6 0.0 copy-done.13
  53.6 0.0 copy-start.3
  53.6 1.2 %fusion.8 = f32[640,128]{1,0:T(8,128)} fusion(bf16[8,128,640]{1,2,0:T(8,128)(2,1)S(1)} %fusion.1, bf16[128,2,8,128]{0,3,2,1:T(8,128)(2,1)S(1)} %bitcast.188), kind=kOutput, calls=%fused_computation.31 | convolution fusion | flops 167854080 | bytes 1900544 | tf_op jit(solution)/shard_map/rqk,qrd->kd/dot_general | solution.py:60
  54.8 1.9 %copy.60 = f32[5,128,128]{1,2,0:T(8,128)} copy(f32[5,128,128]{2,1,0:T(8,128)} %bitcast.196) | data formatting | bytes 655360 | tf_op jit(solution)/shard_map/reshape | solution.py:124
  56.7 2.0 %fusion.3 = bf16[8,128,640]{1,2,0:T(8,128)(2,1)S(1)} fusion(f32[640,128,8]{1,0,2:T(8,128)S(1)} %get-tuple-element.27, f32[8,128]{1,0:T(8,128)} %get-tuple-element.24, f32[8,128]{1,0:T(8,128)} %get-tuple-element.12, f32[8,128]{1,0:T(8,128)} %copy-done.11, pred[128,640]{0,1:T(8,128)(4,1)S(1)} %fusion.12, bf16[128,2,8,128]{0,3,2,1:T(8,128)(2,1)} %bitcast.191, ...), kind=kOutput, calls=%fused_computation.6 | convolution fusion | flops 173015040 | bytes 4452352 | tf_op jit(solution)/shard_map/qrd,kd->rqk/dot_general | solution.py:51
  58.7 1.1 copy-done.1
  59.8 1.2 %fusion.9 = f32[640,128]{1,0:T(8,128)} fusion(bf16[8,128,640]{1,2,0:T(8,128)(2,1)S(1)} %fusion.3, bf16[128,2,8,128]{0,3,2,1:T(8,128)(2,1)S(1)} %bitcast.189), kind=kOutput, calls=%fused_computation.33 | convolution fusion | flops 167854080 | bytes 1900544 | tf_op jit(solution)/shard_map/rqk,qrd->kd/dot_general | solution.py:60
  61.0 1.1 %copy.59 = f32[5,128,128]{1,2,0:T(8,128)S(1)} copy(f32[5,128,128]{2,1,0:T(8,128)} %bitcast.195) | data formatting | bytes 655360 | tf_op jit(solution)/shard_map/reshape | solution.py:124
  62.2 0.0 copy-start.6
  62.2 3.3 %select_convert_fusion.1 = (bf16[640,128,8]{1,0,2:T(8,128)(2,1)S(1)}, bf16[640,128,8]{1,0,2:T(8,128)(2,1)S(1)}) fusion(f32[640,128,8]{1,0,2:T(8,128)S(1)} %get-tuple-element.27, f32[128,8]{0,1:T(8,128)} %bitcast.205, f32[128,8]{0,1:T(8,128)} %bitcast.201, pred[640,128]{1,0:T(8,128)(4,1)S(1)} %copy-done.9, f32[128,8]{0,1:T(8,128)} %bitcast.203, ...), kind=kLoop, calls=%fused_computation.9 | loop fusion | flops 7864320 | bytes 7962624 | tf_op jit(solution)/shard_map/convert_element_type | solution.py:50
  65.4 0.0 copy-start.7
  65.5 0.5 convolution_bitcast_fusion
  66.0 0.5 convolution_bitcast_fusion.1
  66.6 0.1 maximum_bitcast_fusion
  66.7 0.1 fusion.24
  66.8 2.8 %collective-permute-start.7 = (f32[2,128,256]{1,2,0:T(8,128)S(1)}, f32[2,128,256]{1,2,0:T(8,128)S(1)}, u32[]{:S(2)}, u32[]{:S(2)}) collective-permute-start(f32[2,128,256]{1,2,0:T(8,128)S(1)} %get-tuple-element.16), channel_id=1, source_target_pairs={{16,0},{20,4},{24,8},{28,12},{32,16},{36,20},{40,24},{44,28},{48,3... | collective-permute-start | bytes 786440 | tf_op jit(solution)/shard_map/ppermute | solution.py:17
  69.6 2.2 %collective-permute-start.6 = (f32[2,128,256]{1,2,0:T(8,128)S(1)}, f32[2,128,256]{1,2,0:T(8,128)S(1)}, u32[]{:S(2)}, u32[]{:S(2)}) collective-permute-start(f32[2,128,256]{1,2,0:T(8,128)S(1)} %get-tuple-element.17), channel_id=1, source_target_pairs={{12,0},{16,4},{20,8},{24,12},{28,16},{32,20},{36,24},{40,28},{44,3... | collective-permute-start | bytes 786440 | tf_op jit(solution)/shard_map/ppermute | solution.py:17
  71.8 3.7 %collective-permute-start.5 = (f32[2,128,256]{1,2,0:T(8,128)S(1)}, f32[2,128,256]{1,2,0:T(8,128)S(1)}, u32[]{:S(2)}, u32[]{:S(2)}) collective-permute-start(f32[2,128,256]{1,2,0:T(8,128)S(1)} %get-tuple-element.15), channel_id=1, source_target_pairs={{8,0},{12,4},{16,8},{20,12},{24,16},{28,20},{32,24},{36,28},{40,32... | collective-permute-start | bytes 786440 | tf_op jit(solution)/shard_map/ppermute | solution.py:17
  75.5 2.0 %collective-permute-start.4 = (f32[2,128,256]{1,2,0:T(8,128)S(1)}, f32[2,128,256]{1,2,0:T(8,128)S(1)}, u32[]{:S(2)}, u32[]{:S(2)}) collective-permute-start(f32[2,128,256]{1,2,0:T(8,128)S(1)} %get-tuple-element.14), channel_id=1, source_target_pairs={{4,0},{8,4},{12,8},{16,12},{20,16},{24,20},{28,24},{32,28},{36,32}... | collective-permute-start | bytes 786440 | tf_op jit(solution)/shard_map/ppermute | solution.py:17
  77.5 0.4 fusion.10
  77.9 1.9 %collective-permute-done.7 = f32[2,128,256]{1,2,0:T(8,128)S(1)} collective-permute-done((f32[2,128,256]{1,2,0:T(8,128)S(1)}, f32[2,128,256]{1,2,0:T(8,128)S(1)}, u32[]{:S(2)}, u32[]{:S(2)}) %collective-permute-start.7) | collective-permute-done | bytes 262176 | tf_op jit(solution)/shard_map/ppermute | solution.py:17
  79.8 6.0 %collective-permute-done.6 = f32[2,128,256]{1,2,0:T(8,128)S(1)} collective-permute-done((f32[2,128,256]{1,2,0:T(8,128)S(1)}, f32[2,128,256]{1,2,0:T(8,128)S(1)}, u32[]{:S(2)}, u32[]{:S(2)}) %collective-permute-start.6) | collective-permute-done | bytes 262176 | tf_op jit(solution)/shard_map/ppermute | solution.py:17
  85.8 5.5 %collective-permute-done.5 = f32[2,128,256]{1,2,0:T(8,128)S(1)} collective-permute-done((f32[2,128,256]{1,2,0:T(8,128)S(1)}, f32[2,128,256]{1,2,0:T(8,128)S(1)}, u32[]{:S(2)}, u32[]{:S(2)}) %collective-permute-start.5) | collective-permute-done | bytes 262176 | tf_op jit(solution)/shard_map/ppermute | solution.py:17
  91.3 3.2 %collective-permute-done.4 = f32[2,128,256]{1,2,0:T(8,128)S(1)} collective-permute-done((f32[2,128,256]{1,2,0:T(8,128)S(1)}, f32[2,128,256]{1,2,0:T(8,128)S(1)}, u32[]{:S(2)}, u32[]{:S(2)}) %collective-permute-start.4) | collective-permute-done | bytes 262176 | tf_op jit(solution)/shard_map/ppermute | solution.py:17
  94.6 0.1 fusion.22
  94.7 0.7 copy.67
  95.4 3.5 %all-to-all-start = ((bf16[4,32,256]{2,1,0:T(8,128)(2,1)}), bf16[4,32,256]{2,1,0:T(8,128)(2,1)S(1)}, u32[]{:S(2)}, u32[]{:S(2)}) async-start(bf16[4,32,256]{2,1,0:T(8,128)(2,1)} %bitcast.51), calls=%async_computation | async-start | bytes 131072 | tf_op jit(solution)/shard_map/all_to_all | solution.py:137
  99.0 0.4 fusion.11
  99.4 0.7 copy.69
  100.1 3.3 %all-to-all-done = bf16[4,32,256]{2,1,0:T(8,128)(2,1)S(1)} async-done(((bf16[4,32,256]{2,1,0:T(8,128)(2,1)}), bf16[4,32,256]{2,1,0:T(8,128)(2,1)S(1)}, u32[]{:S(2)}, u32[]{:S(2)}) %all-to-all-start) | async-done | bytes 65568 | tf_op jit(solution)/shard_map/all_to_all | solution.py:137
  103.4 3.3 %all-to-all-start.1 = ((bf16[4,32,256]{2,1,0:T(8,128)(2,1)}), bf16[4,32,256]{2,1,0:T(8,128)(2,1)S(1)}, u32[]{:S(2)}, u32[]{:S(2)}) async-start(bf16[4,32,256]{2,1,0:T(8,128)(2,1)} %bitcast.53), calls=%async_computation.1 | async-start | bytes 131072 | tf_op jit(solution)/shard_map/all_to_all | solution.py:140
  106.7 0.1 pad_maximum_fusion
  106.8 1.0 copy.71
  107.8 0.6 copy.92
  108.4 2.9 %all-to-all-done.1 = bf16[4,32,256]{2,1,0:T(8,128)(2,1)S(1)} async-done(((bf16[4,32,256]{2,1,0:T(8,128)(2,1)}), bf16[4,32,256]{2,1,0:T(8,128)(2,1)S(1)}, u32[]{:S(2)}, u32[]{:S(2)}) %all-to-all-start.1) | async-done | bytes 65568 | tf_op jit(solution)/shard_map/all_to_all | solution.py:140
  111.4 0.6 copy.93
  (29 shorter events, 0.2 us)
Async XLA Ops:
  0.6 46.4 %copy-start.8 = (bf16[128,2048]{1,0:T(8,128)(2,1)S(1)}, bf16[128,2048]{1,0:T(8,128)(2,1)}, u32[]{:S(2)}) copy-start(bf16[128,2048]{1,0:T(8,128)(2,1)} %param.9) | copy-start | bytes 1572868
  21.0 27.0 %collective-permute-start = (bf16[2,128,256]{2,1,0:T(8,128)(2,1)S(1)}, bf16[2,128,256]{2,1,0:T(8,128)(2,1)S(1)}, u32[]{:S(2)}, u32[]{:S(2)}) collective-permute-start(bf16[2,128,256]{2,1,0:T(8,128)(2,1)S(1)} %pad_maximum_fusion.2), channel_id=1, source_target_pairs={{0,16},{4,20},{8,24},{12,28},{16,32},{20,36},{24,40},{28,44},{32,4... | collective-permute-start | bytes 393224 | tf_op jit(solution)/shard_map/ppermute | solution.py:17
  26.6 21.4 %collective-permute-start.1 = (bf16[2,128,256]{2,1,0:T(8,128)(2,1)S(1)}, bf16[2,128,256]{2,1,0:T(8,128)(2,1)S(1)}, u32[]{:S(2)}, u32[]{:S(2)}) collective-permute-start(bf16[2,128,256]{2,1,0:T(8,128)(2,1)S(1)} %pad_maximum_fusion.2), channel_id=1, source_target_pairs={{0,12},{4,16},{8,20},{12,24},{16,28},{20,32},{24,36},{28,40},{32,4... | collective-permute-start | bytes 393224 | tf_op jit(solution)/shard_map/ppermute | solution.py:17
  36.5 11.6 %collective-permute-start.2 = (bf16[2,128,256]{2,1,0:T(8,128)(2,1)S(1)}, bf16[2,128,256]{2,1,0:T(8,128)(2,1)S(1)}, u32[]{:S(2)}, u32[]{:S(2)}) collective-permute-start(bf16[2,128,256]{2,1,0:T(8,128)(2,1)S(1)} %pad_maximum_fusion.2), channel_id=1, source_target_pairs={{0,8},{4,12},{8,16},{12,20},{16,24},{20,28},{24,32},{28,36},{32,40... | collective-permute-start | bytes 393224 | tf_op jit(solution)/shard_map/ppermute | solution.py:17
  40.0 8.1 %collective-permute-start.3 = (bf16[2,128,256]{2,1,0:T(8,128)(2,1)S(1)}, bf16[2,128,256]{2,1,0:T(8,128)(2,1)S(1)}, u32[]{:S(2)}, u32[]{:S(2)}) collective-permute-start(bf16[2,128,256]{2,1,0:T(8,128)(2,1)S(1)} %pad_maximum_fusion.2), channel_id=1, source_target_pairs={{0,4},{4,8},{8,12},{12,16},{16,20},{20,24},{24,28},{28,32},{32,36}... | collective-permute-start | bytes 393224 | tf_op jit(solution)/shard_map/ppermute | solution.py:17
  48.2 3.6 %copy-start.10 = (bf16[640,256]{1,0:T(8,128)(2,1)}, bf16[640,256]{1,0:T(8,128)(2,1)S(1)}, u32[]{:S(2)}) copy-start(bf16[640,256]{1,0:T(8,128)(2,1)S(1)} %get-tuple-element.18) | copy-start | bytes 983044
  48.7 0.6 copy-start.11
  51.1 2.5 %copy-start = (f32[640,128,8]{1,0,2:T(8,128)}, f32[640,128,8]{1,0,2:T(8,128)S(1)}, u32[]{:S(2)}) copy-start(f32[640,128,8]{1,0,2:T(8,128)S(1)} %get-tuple-element.28) | copy-start | bytes 7864324
  51.1 2.5 %copy-start.12 = (f32[8,128]{1,0:T(8,128)}, f32[8,128]{1,0:T(8,128)S(1)}, u32[]{:S(2)}) copy-start(f32[8,128]{1,0:T(8,128)S(1)} %get-tuple-element.13) | copy-start | bytes 12292
  51.1 1.4 %copy-start.5 = (bf16[128,2048]{0,1:T(8,128)(2,1)S(1)}, bf16[128,2048]{0,1:T(8,128)(2,1)}, u32[]{:S(2)}) copy-start(bf16[128,2048]{0,1:T(8,128)(2,1)} %copy.51) | copy-start | bytes 1572868
  51.1 1.4 %copy-start.14 = (f32[8,128]{1,0:T(8,128)S(1)}, f32[8,128]{1,0:T(8,128)}, u32[]{:S(2)}) copy-start(f32[8,128]{1,0:T(8,128)} %get-tuple-element.25) | copy-start | bytes 12292
  51.7 1.8 %copy-start.13 = (f32[8,128]{1,0:T(8,128)}, f32[8,128]{1,0:T(8,128)S(1)}, u32[]{:S(2)}) copy-start(f32[8,128]{1,0:T(8,128)S(1)} %select_reduce_fusion) | copy-start | bytes 12292
  53.6 1.2 %copy-start.3 = (bf16[8,128,640]{1,2,0:T(8,128)(2,1)}, bf16[8,128,640]{1,2,0:T(8,128)(2,1)S(1)}, u32[]{:S(2)}) copy-start(bf16[8,128,640]{1,2,0:T(8,128)(2,1)S(1)} %fusion.1) | copy-start | bytes 3932164
  58.7 1.1 copy-start.1
  59.8 2.4 %copy-start.9 = (pred[640,128]{1,0:T(8,128)(4,1)S(1)}, pred[640,128]{1,0:T(8,128)(4,1)}, u32[]{:S(2)}) copy-start(pred[640,128]{1,0:T(8,128)(4,1)} %fusion.13) | copy-start | bytes 245764
  62.2 3.3 %copy-start.6 = (bf16[128,2048]{0,1:T(8,128)(2,1)S(1)}, bf16[128,2048]{0,1:T(8,128)(2,1)}, u32[]{:S(2)}) copy-start(bf16[128,2048]{0,1:T(8,128)(2,1)} %copy.51) | copy-start | bytes 1572868
  65.4 1.1 copy-start.7
  66.6 10.9 %copy-start.4 = (bf16[8,128,640]{1,2,0:T(8,128)(2,1)S(1)}, bf16[8,128,640]{1,2,0:T(8,128)(2,1)}, u32[]{:S(2)}) copy-start(bf16[8,128,640]{1,2,0:T(8,128)(2,1)} %copy-done.3) | copy-start | bytes 3932164
  66.8 32.2 %copy-start.2 = (bf16[8,128,640]{1,2,0:T(8,128)(2,1)S(1)}, bf16[8,128,640]{1,2,0:T(8,128)(2,1)}, u32[]{:S(2)}) copy-start(bf16[8,128,640]{1,2,0:T(8,128)(2,1)} %copy-done.1) | copy-start | bytes 3932164
  66.8 13.1 %collective-permute-start.7 = (f32[2,128,256]{1,2,0:T(8,128)S(1)}, f32[2,128,256]{1,2,0:T(8,128)S(1)}, u32[]{:S(2)}, u32[]{:S(2)}) collective-permute-start(f32[2,128,256]{1,2,0:T(8,128)S(1)} %get-tuple-element.16), channel_id=1, source_target_pairs={{16,0},{20,4},{24,8},{28,12},{32,16},{36,20},{40,24},{44,28},{48,3... | collective-permute-start | bytes 786440 | tf_op jit(solution)/shard_map/ppermute | solution.py:17
  69.6 16.2 %collective-permute-start.6 = (f32[2,128,256]{1,2,0:T(8,128)S(1)}, f32[2,128,256]{1,2,0:T(8,128)S(1)}, u32[]{:S(2)}, u32[]{:S(2)}) collective-permute-start(f32[2,128,256]{1,2,0:T(8,128)S(1)} %get-tuple-element.17), channel_id=1, source_target_pairs={{12,0},{16,4},{20,8},{24,12},{28,16},{32,20},{36,24},{40,28},{44,3... | collective-permute-start | bytes 786440 | tf_op jit(solution)/shard_map/ppermute | solution.py:17
  71.8 19.5 %collective-permute-start.5 = (f32[2,128,256]{1,2,0:T(8,128)S(1)}, f32[2,128,256]{1,2,0:T(8,128)S(1)}, u32[]{:S(2)}, u32[]{:S(2)}) collective-permute-start(f32[2,128,256]{1,2,0:T(8,128)S(1)} %get-tuple-element.15), channel_id=1, source_target_pairs={{8,0},{12,4},{16,8},{20,12},{24,16},{28,20},{32,24},{36,28},{40,32... | collective-permute-start | bytes 786440 | tf_op jit(solution)/shard_map/ppermute | solution.py:17
  75.5 19.1 %collective-permute-start.4 = (f32[2,128,256]{1,2,0:T(8,128)S(1)}, f32[2,128,256]{1,2,0:T(8,128)S(1)}, u32[]{:S(2)}, u32[]{:S(2)}) collective-permute-start(f32[2,128,256]{1,2,0:T(8,128)S(1)} %get-tuple-element.14), channel_id=1, source_target_pairs={{4,0},{8,4},{12,8},{16,12},{20,16},{24,20},{28,24},{32,28},{36,32}... | collective-permute-start | bytes 786440 | tf_op jit(solution)/shard_map/ppermute | solution.py:17
  95.4 8.0 %all-to-all-start = ((bf16[4,32,256]{2,1,0:T(8,128)(2,1)}), bf16[4,32,256]{2,1,0:T(8,128)(2,1)S(1)}, u32[]{:S(2)}, u32[]{:S(2)}) async-start(bf16[4,32,256]{2,1,0:T(8,128)(2,1)} %bitcast.51), calls=%async_computation | async-start | bytes 131072 | tf_op jit(solution)/shard_map/all_to_all | solution.py:137
  103.4 7.9 %all-to-all-start.1 = ((bf16[4,32,256]{2,1,0:T(8,128)(2,1)}), bf16[4,32,256]{2,1,0:T(8,128)(2,1)S(1)}, u32[]{:S(2)}, u32[]{:S(2)}) async-start(bf16[4,32,256]{2,1,0:T(8,128)(2,1)} %bitcast.53), calls=%async_computation.1 | async-start | bytes 131072 | tf_op jit(solution)/shard_map/all_to_all | solution.py:140
where the time goes:
time: 113 us; the launch traced here: 112 us
  starting transfers between devices  38.3 us (34%)
  waiting for transfers between devices  22.9 us (20%)
  blocking collectives  20.3 us (18%)
  local copies, waits for them, and re-layouts  14.5 us (13%)
  matrix products  9.69 us (9%)
  other arithmetic  5.19 us (5%)
    ppermute x8, starting transfers between devices, passed_along(): return lax.ppermute(block, axis, route)  31.5 us
    ppermute x8, waiting for transfers between devices, passed_along(): return lax.ppermute(block, axis, route)  16.7 us
    all_gather x1, blocking collectives, on_device(): lax.all_gather(values, 'hd', axis=0, tiled=True)  10.8 us
    all_gather x1, blocking collectives, on_device(): lax.all_gather(keys, 'hd', axis=0, tiled=True)  9.57 us
    unnamed x37, local copies, waits for them, and re-layouts  5.78 us
    all_to_all x1, starting transfers between devices, on_device(): lax.all_to_all(summed[0].astype(jnp.bfloat16), 'hd', split_axis=0, concat...  3.52 us
    all_to_all x1, waiting for transfers between devices, on_device(): lax.all_to_all(summed[0].astype(jnp.bfloat16), 'hd', split_axis=0, concat...  3.33 us
    all_to_all x1, starting transfers between devices, on_device(): lax.all_to_all(summed[1].astype(jnp.bfloat16), 'hd', split_axis=0, concat...  3.28 us
  transfers between devices with their start and end apart: 10, of which 6 were waited for; matrix products, arithmetic and copies ran while one was open for 8% of the time, Pallas kernels for 0%

commit v1 on v0

v1 whole, which is shorter than its diff:
```python
import math

import jax
import jax.numpy as jnp
from jax import lax
from jax.experimental import pallas as pl
from jax.experimental.pallas import tpu as pltpu
from jax.sharding import PartitionSpec as P

MESH = pl.DeviceIdType.MESH
HD = 128
HEADS = 8
TOK = 128
PAIR = 2 * TOK
SPAN = 3 * PAIR
SEEN = 5 * TOK
HALF = HEADS * HD
PIECE = 32
FILL = -1e30
SCALE = 1.0 / math.sqrt(HD)
LOG2E = math.log2(math.e)
PARTNERS = [(0, 2), (1, 2), (0, 1), (0, 3), (1, 1), (1, 3), (1, 0)]
NT = (((1,), (1,)), ((), ()))


def aligned(index, size):
    return pl.multiple_of(index * size, size)


def kernel(
    query, keys, values, grad_out, delta, segments,
    dq_out, dk_out, dv_out,
    qb, gb, dt, sb, kb, vb, kt, scores, gweights, probs, dscores, bias,
    own, outbox, inbox, totals, dqs,
    local_sem, kv_send, kv_recv, pair_send, pair_recv,
    shift_send, shift_recv, back_send, back_recv, fin_send, fin_recv, dq_send, dq_recv,
):
    tok, hd = lax.axis_index("tok"), lax.axis_index("hd")
    chips = lax.axis_size("tok") // 2
    rows_y = lax.axis_size("hd")
    core, chip = lax.rem(tok, 2), lax.div(tok, 2)
    other = 1 - core

    def local(index, src, dst):
        copy = pltpu.make_async_copy(src, dst, local_sem.at[index])
        copy.start()
        return copy

    def remote(src, dst, send, recv, to_tok, to_hd):
        return pltpu.make_async_remote_copy(
            src_ref=src, dst_ref=dst, send_sem=send, recv_sem=recv,
            device_id=(to_tok, to_hd), device_id_type=MESH,
        )

    def partner(k):
        cross, step = PARTNERS[k]
        pcore = other if cross else core
        return pcore, lax.rem(hd + step, rows_y)

    mine = pl.ds(aligned(2 * hd + core, HD), HD)
    slot = pl.ds(pl.multiple_of((4 + core) * TOK + PIECE * hd, PIECE), PIECE)
    half = pl.ds(aligned(core, HALF), HALF)
    far_half = pl.ds(aligned(other, HALF), HALF)
    my_rows = pl.ds(aligned(core, TOK), TOK)
    loc_k = local(0, keys.at[:, mine], kb.at[slot])
    loc_v = local(1, values.at[:, mine], vb.at[slot])
    loc_s = local(2, segments, sb)

    barrier = pltpu.get_barrier_semaphore()
    for k in range(len(PARTNERS)):
        pcore, ph = partner(k)
        pl.semaphore_signal(barrier, 1, device_id=(2 * chip + pcore, ph), device_id_type=MESH)
    for step in (1, 2):
        @pl.when(chip + step < chips)
        def _(step=step):
            pl.semaphore_signal(barrier, 1, device_id=(tok + 2 * step, hd), device_id_type=MESH)

        @pl.when(chip >= step)
        def _(step=step):
            pl.semaphore_signal(barrier, 1, device_id=(tok - 2 * step, hd), device_id_type=MESH)

    near = sum(
        jnp.where(c, 1, 0)
        for c in (chip >= 1, chip >= 2, chip + 1 < chips, chip + 2 < chips)
    )
    pl.semaphore_wait(barrier, len(PARTNERS) + near)

    kv_copies = []
    for which, (source, target) in enumerate(((keys, kb), (values, vb))):
        for k in range(len(PARTNERS)):
            pcore, ph = partner(k)
            cols = pl.ds(aligned(2 * ph + pcore, HD), HD)
            copy = remote(
                source.at[:, cols], target.at[slot],
                kv_send.at[which, k], kv_recv.at[which, k], 2 * chip + pcore, ph,
            )
            copy.start()
            kv_copies.append(copy)
    pair_copies = []
    for k, (src, dst) in enumerate((
        (query.at[:, far_half], qb.at[my_rows]),
        (grad_out.at[:, far_half], gb.at[my_rows]),
        (delta, dt.at[core]),
    )):
        copy = remote(src, dst, pair_send.at[k], pair_recv.at[k], 2 * chip + other, hd)
        copy.start()
        pair_copies.append(copy)
    loc_q = local(3, query.at[:, half], qb.at[my_rows])
    loc_g = local(4, grad_out.at[:, half], gb.at[my_rows])
    loc_d = local(5, delta, dt.at[core])

    for step in (1, 2):
        @pl.when(chip < step)
        def _(step=step):
            empty = pl.ds((2 - step) * PAIR, PAIR)
            kb[empty, :] = jnp.zeros((PAIR, HD), kb.dtype)
            vb[empty, :] = jnp.zeros((PAIR, HD), vb.dtype)

        @pl.when(chip + step >= chips)
        def _(step=step):
            inbox[step - 1] = jnp.zeros(inbox.shape[1:], inbox.dtype)

    loc_s.wait()

    def ids(shard):
        row = sb[pl.ds(jnp.maximum(shard, 0), 1), :]
        return jnp.where(shard < 0, -1, row)

    shards = [2 * chip - 4 + s for s in range(6)]
    rows = [ids(s) for s in shards]
    tall = [jnp.transpose(jnp.broadcast_to(r, (TOK, TOK))) for r in rows]
    key_at = lax.broadcasted_iota(jnp.int32, (TOK, TOK), 0)
    query_at = lax.broadcasted_iota(jnp.int32, (TOK, TOK), 1)
    for b in range(2):
        for s in range(5):
            allowed = tall[b + s] == rows[4 + b]
            if s == 4:
                allowed = allowed & (key_at <= query_at)
            bias[b, s * TOK : (s + 1) * TOK, :] = jnp.where(allowed, 0.0, FILL)
    nothing = jnp.zeros((TOK, TOK), probs.dtype)
    for head in range(HEADS):
        for ref in (probs, dscores):
            ref[SEEN:SPAN, head * PAIR : head * PAIR + TOK] = nothing
            ref[0:TOK, head * PAIR + TOK : (head + 1) * PAIR] = nothing

    shift = [[[None] * 2 for _ in range(2)] for _ in range(2)]
    for which, (ref, loc) in enumerate(((kb, loc_k), (vb, loc_v))):
        loc.wait()
        for k in range(len(PARTNERS)):
            kv_copies[which * len(PARTNERS) + k].wait_recv()
        for step in (1, 2):
            copy = remote(
                ref.at[pl.ds(2 * PAIR, PAIR)], ref.at[pl.ds((2 - step) * PAIR, PAIR)],
                shift_send.at[step - 1, which], shift_recv.at[step - 1, which],
                tok + 2 * step, hd,
            )
            shift[step - 1][which] = copy

            @pl.when(chip + step < chips)
            def _(copy=copy):
                copy.start()

    loc_q.wait()
    loc_g.wait()
    loc_d.wait()
    for copy in pair_copies:
        copy.wait_recv()

    def products(block):
        span = slice(block * PAIR, (block + 1) * PAIR)

        def body(head, _):
            cols = pl.ds(aligned(head, HD), HD)
            scores[head, span, :] = lax.dot_general(
                kb[span, :], qb[:, cols], NT, preferred_element_type=jnp.float32
            )
            gweights[head, span, :] = lax.dot_general(
                vb[span, :], gb[:, cols], NT, preferred_element_type=jnp.float32
            )
            return 0

        lax.fori_loop(0, HEADS, body, 0)
        kt[:, span] = jnp.transpose(kb[span, :])

    products(2)
    for step in (1, 2):
        @pl.when(chip >= step)
        def _(step=step):
            for which in range(2):
                shift[step - 1][which].wait_recv()

        products(2 - step)

    def softmax(head, _):
        for b in range(2):
            span = slice(b * TOK, b * TOK + SEEN)
            lanes = slice(b * TOK, (b + 1) * TOK)
            raw = scores[head, span, lanes] + bias[b]
            top = jnp.max(raw, axis=0, keepdims=True)
            grown = jnp.exp2((raw - top) * (SCALE * LOG2E))
            total = jnp.sum(grown, axis=0, keepdims=True)
            weights = grown * (1.0 / total)
            row_delta = dt[b, pl.ds(core * HEADS + head, 1), :]
            grads = weights * (gweights[head, span, lanes] - row_delta)
            cols = pl.ds(pl.multiple_of(head * PAIR + b * TOK, TOK), TOK)
            probs[span, cols] = weights.astype(probs.dtype)
            dscores[span, cols] = grads.astype(dscores.dtype)
        return 0

    lax.fori_loop(0, HEADS, softmax, 0)

    def key_value_grads(block):
        span = slice(block * PAIR, (block + 1) * PAIR)
        dk = jnp.zeros((PAIR, HD), jnp.float32)
        dv = jnp.zeros((PAIR, HD), jnp.float32)
        for head in range(HEADS):
            lanes = slice(head * PAIR, (head + 1) * PAIR)
            cols = slice(head * HD, (head + 1) * HD)
            dk += jnp.dot(dscores[span, lanes], qb[:, cols], preferred_element_type=jnp.float32)
            dv += jnp.dot(probs[span, lanes], gb[:, cols], preferred_element_type=jnp.float32)
        return dk * SCALE, dv

    back = [None, None]
    for step in (2, 1):
        dk, dv = key_value_grads(2 - step)
        outbox[step - 1, 0] = dk.astype(outbox.dtype)
        outbox[step - 1, 1] = dv.astype(outbox.dtype)
        copy = remote(
            outbox.at[step - 1], inbox.at[step - 1],
            back_send.at[step - 1], back_recv.at[step - 1], tok - 2 * step, hd,
        )
        back[step - 1] = copy

        @pl.when(chip >= step)
        def _(copy=copy):
            copy.start()

    dk, dv = key_value_grads(2)
    own[0] = dk
    own[1] = dv

    def query_grads(head, _):
        lanes = pl.ds(aligned(head, PAIR), PAIR)
        turned = jnp.dot(kt[...], dscores[:, lanes], preferred_element_type=jnp.float32)
        turned = turned * SCALE
        cols = pl.ds(aligned(head, HD), HD)
        for b in range(2):
            block = jnp.transpose(turned[:, b * TOK : (b + 1) * TOK])
            dqs[b, :, cols] = block.astype(dqs.dtype)
        return 0

    lax.fori_loop(0, HEADS, query_grads, 0)
    dq_copy = remote(
        dqs.at[other], dq_out.at[:, half], dq_send.at[0], dq_recv.at[0], 2 * chip + other, hd
    )
    dq_copy.start()
    loc_dq = local(6, dqs.at[core], dq_out.at[:, half])

    for step in (1, 2):
        @pl.when(chip + step < chips)
        def _(step=step):
            back[step - 1].wait_recv()

    for which in range(2):
        total = own[which]
        for step in range(2):
            total += inbox[step, which].astype(jnp.float32)
        totals[which] = total.astype(totals.dtype)
    fin_copies = []
    for which, out in enumerate((dk_out, dv_out)):
        for k in range(len(PARTNERS)):
            pcore, ph = partner(k)
            src_rows = pl.ds(pl.multiple_of(pcore * TOK + PIECE * ph, PIECE), PIECE)
            copy = remote(
                totals.at[which, src_rows], out.at[:, mine],
                fin_send.at[which, k], fin_recv.at[which, k], 2 * chip + pcore, ph,
            )
            copy.start()
            fin_copies.append(copy)
    own_rows = pl.ds(pl.multiple_of(core * TOK + PIECE * hd, PIECE), PIECE)
    loc_dk = local(7, totals.at[0, own_rows], dk_out.at[:, mine])
    loc_dv = local(8, totals.at[1, own_rows], dv_out.at[:, mine])

    for copy in kv_copies + pair_copies:
        copy.wait_send()
    for step in (1, 2):
        @pl.when(chip + step < chips)
        def _(step=step):
            for which in range(2):
                shift[step - 1][which].wait_send()

        @pl.when(chip >= step)
        def _(step=step):
            back[step - 1].wait_send()

    loc_dq.wait()
    loc_dk.wait()
    loc_dv.wait()
    dq_copy.wait()
    for copy in fin_copies:
        copy.wait()


def on_device(query, keys, values, grad_out, delta, segments):
    low, full = jnp.bfloat16, jnp.float32
    tokens = query.shape[0]
    dma = pltpu.SemaphoreType.DMA
    partners = len(PARTNERS)
    return tuple(pl.pallas_call(
        kernel,
        out_shape=(
            pltpu.VMEM(query.shape, low),
            pltpu.VMEM(keys.shape, low),
            pltpu.VMEM(values.shape, low),
        ),
        in_specs=[pl.BlockSpec(memory_space=pl.ANY)] * 6,
        out_specs=[pl.BlockSpec(memory_space=pltpu.VMEM)] * 3,
        scratch_shapes=[
            pltpu.VMEM((PAIR, HALF), low),
            pltpu.VMEM((PAIR, HALF), low),
            pltpu.VMEM((2,) + delta.shape[::-1], full),
            pltpu.VMEM((segments.shape[0] // TOK, TOK), jnp.int32),
            pltpu.VMEM((SPAN, HD), low),
            pltpu.VMEM((SPAN, HD), low),
            pltpu.VMEM((HD, SPAN), low),
            pltpu.VMEM((HEADS, SPAN, PAIR), full),
            pltpu.VMEM((HEADS, SPAN, PAIR), full),
            pltpu.VMEM((SPAN, HEADS * PAIR), low),
            pltpu.VMEM((SPAN, HEADS * PAIR), low),
            pltpu.VMEM((2, SEEN, TOK), full),
            pltpu.VMEM((2, PAIR, HD), full),
            pltpu.VMEM((2, 2, PAIR, HD), low),
            pltpu.VMEM((2, 2, PAIR, HD), low),
            pltpu.VMEM((2, PAIR, HD), low),
            pltpu.VMEM((2, tokens, HALF), low),
            dma((9,)),
            dma((2, partners)), dma((2, partners)),
            dma((3,)), dma((3,)),
            dma((2, 2)), dma((2, 2)),
            dma((2,)), dma((2,)),
            dma((2, partners)), dma((2, partners)),
            dma((1,)), dma((1,)),
        ],
        compiler_params=pltpu.CompilerParams(
            collective_id=0, has_side_effects=True, vmem_limit_bytes=62 * 2**20
        ),
    )(query, keys, values, grad_out, delta.T, segments.reshape(-1, TOK)))


def solution(mesh):
    return jax.shard_map(
        on_device,
        mesh=mesh,
        in_specs=(
            P("tok", "hd"),
            P(("tok", "hd"), None),
            P(("tok", "hd"), None),
            P("tok", "hd"),
            P("tok", "hd"),
            P(),
        ),
        out_specs=(P("tok", "hd"), P(("tok", "hd"), None), P(("tok", "hd"), None)),
        check_vma=False,
    )
```

time: 113 us -> 42.6 us (0.38)
  the two profiles are of different devices: /device:TPU:103 before, /device:TPU:231 now
where the time goes in v1:
time: 42.6 us; the launch traced here: 42.5 us
  Pallas kernels  39.8 us (93%)
  local copies, waits for them, and re-layouts  2.05 us (5%)
  between operations  0.64 us (2%)
    pallas_call x1, Pallas kernels, on_device(): pl.pallas_call(kernel, out_shape=(pltpu.VMEM(query.shape, low), pltpu.VME...  39.8 us
    unnamed x3, local copies, waits for them, and re-layouts  2.05 us

profile of v1, /device:TPU:231, one launch (start us, length us, event | category | flops | bytes accessed | tf_op | source)
XLA Modules:
  0.0 42.5 jit_solution(3473888744542220400)
XLA Ops:
  0.6 39.8 %shard_map.85 = (bf16[128,2048]{1,0:T(8,128)(2,1)S(1)}, bf16[32,1024]{1,0:T(8,128)(2,1)S(1)}, bf16[32,1024]{1,0:T(8,128)(2,1)S(1)}) custom-call(bf16[128,2048]{1,0:T(8,128)(2,1)} %query.1, bf16[32,1024]{1,0:T(8,128)(2,1)} %keys.1, bf16[32,1024]{1,0:T(8,128)(2,1)} %values.1, bf16[128,2048]{1,0:T(8,128)(2,1)} %grad_out.1, f32[16,128]{1,0:T(8,128)} %bitcast.3, ...), custom_call_target="tpu_custom_call" | custom-call | tf_op jit(solution)/shard_map/pallas_call | solution.py:309
  40.4 0.8 %copy.12 = bf16[128,2048]{1,0:T(8,128)(2,1)} copy(bf16[128,2048]{1,0:T(8,128)(2,1)S(1)} %get-tuple-element.3) | data formatting | bytes 1048576
  41.2 0.6 %copy.13 = bf16[32,1024]{1,0:T(8,128)(2,1)} copy(bf16[32,1024]{1,0:T(8,128)(2,1)S(1)} %get-tuple-element.4) | data formatting | bytes 131072
  41.9 0.6 %copy.14 = bf16[32,1024]{1,0:T(8,128)(2,1)} copy(bf16[32,1024]{1,0:T(8,128)(2,1)S(1)} %get-tuple-element.5) | data formatting | bytes 131072

commit v2 on v1

--- a/solution.py
+++ b/solution.py
@@ -29,8 +29,8 @@
 
 def kernel(
     query, keys, values, grad_out, delta, segments,
-    dq_out, dk_out, dv_out,
-    qb, gb, dt, sb, kb, vb, kt, scores, gweights, probs, dscores, bias,
+    dq_out, dkv_out,
+    stage, qb, gb, dt, sb, kv, kt, scores, gweights, probs, dscores, bias,
     own, outbox, inbox, totals, dqs,
     local_sem, kv_send, kv_recv, pair_send, pair_recv,
     shift_send, shift_recv, back_send, back_recv, fin_send, fin_recv, dq_send, dq_recv,
@@ -62,8 +62,7 @@
     half = pl.ds(aligned(core, HALF), HALF)
     far_half = pl.ds(aligned(other, HALF), HALF)
     my_rows = pl.ds(aligned(core, TOK), TOK)
-    loc_k = local(0, keys.at[:, mine], kb.at[slot])
-    loc_v = local(1, values.at[:, mine], vb.at[slot])
+    loc_stage = [local(0, keys, stage.at[0]), local(1, values, stage.at[1])]
     loc_s = local(2, segments, sb)
 
     barrier = pltpu.get_barrier_semaphore()
@@ -85,17 +84,19 @@
     )
     pl.semaphore_wait(barrier, len(PARTNERS) + near)
 
+    for copy in loc_stage:
+        copy.wait()
     kv_copies = []
-    for which, (source, target) in enumerate(((keys, kb), (values, vb))):
-        for k in range(len(PARTNERS)):
-            pcore, ph = partner(k)
-            cols = pl.ds(aligned(2 * ph + pcore, HD), HD)
-            copy = remote(
-                source.at[:, cols], target.at[slot],
-                kv_send.at[which, k], kv_recv.at[which, k], 2 * chip + pcore, ph,
-            )
-            copy.start()
-            kv_copies.append(copy)
+    for k in range(len(PARTNERS)):
+        pcore, ph = partner(k)
+        cols = pl.ds(aligned(2 * ph + pcore, HD), HD)
+        copy = remote(
+            stage.at[:, :, cols], kv.at[:, slot],
+            kv_send.at[k], kv_recv.at[k], 2 * chip + pcore, ph,
+        )
+        copy.start()
+        kv_copies.append(copy)
+    loc_kv = local(7, stage.at[:, :, mine], kv.at[:, slot])
     pair_copies = []
     for k, (src, dst) in enumerate((
         (query.at[:, far_half], qb.at[my_rows]),
@@ -113,8 +114,7 @@
         @pl.when(chip < step)
         def _(step=step):
             empty = pl.ds((2 - step) * PAIR, PAIR)
-            kb[empty, :] = jnp.zeros((PAIR, HD), kb.dtype)
-            vb[empty, :] = jnp.zeros((PAIR, HD), vb.dtype)
+            kv[:, empty, :] = jnp.zeros((2, PAIR, HD), kv.dtype)
 
         @pl.when(chip + step >= chips)
         def _(step=step):
@@ -144,13 +144,14 @@
             ref[0:TOK, head * PAIR + TOK : (head + 1) * PAIR] = nothing
 
     shift = [[[None] * 2 for _ in range(2)] for _ in range(2)]
-    for which, (ref, loc) in enumerate(((kb, loc_k), (vb, loc_v))):
-        loc.wait()
-        for k in range(len(PARTNERS)):
-            kv_copies[which * len(PARTNERS) + k].wait_recv()
-        for step in (1, 2):
+    loc_kv.wait()
+    for copy in kv_copies:
+        copy.wait_recv()
+    for which in range(2):
+        for step in (2, 1):
             copy = remote(
-                ref.at[pl.ds(2 * PAIR, PAIR)], ref.at[pl.ds((2 - step) * PAIR, PAIR)],
+                kv.at[which, pl.ds(2 * PAIR, PAIR)],
+                kv.at[which, pl.ds((2 - step) * PAIR, PAIR)],
                 shift_send.at[step - 1, which], shift_recv.at[step - 1, which],
                 tok + 2 * step, hd,
             )
@@ -172,15 +173,15 @@
         def body(head, _):
             cols = pl.ds(aligned(head, HD), HD)
             scores[head, span, :] = lax.dot_general(
-                kb[span, :], qb[:, cols], NT, preferred_element_type=jnp.float32
+                kv[0, span, :], qb[:, cols], NT, preferred_element_type=jnp.float32
             )
             gweights[head, span, :] = lax.dot_general(
-                vb[span, :], gb[:, cols], NT, preferred_element_type=jnp.float32
+                kv[1, span, :], gb[:, cols], NT, preferred_element_type=jnp.float32
             )
             return 0
 
-        lax.fori_loop(0, HEADS, body, 0)
-        kt[:, span] = jnp.transpose(kb[span, :])
+        lax.fori_loop(0, HEADS, body, 0, unroll=HEADS)
+        kt[:, span] = jnp.transpose(kv[0, span, :])
 
     products(2)
     for step in (1, 2):
@@ -207,7 +208,7 @@
             dscores[span, cols] = grads.astype(dscores.dtype)
         return 0
 
-    lax.fori_loop(0, HEADS, softmax, 0)
+    lax.fori_loop(0, HEADS, softmax, 0, unroll=HEADS)
 
     def key_value_grads(block):
         span = slice(block * PAIR, (block + 1) * PAIR)
@@ -249,7 +250,7 @@
             dqs[b, :, cols] = block.astype(dqs.dtype)
         return 0
 
-    lax.fori_loop(0, HEADS, query_grads, 0)
+    lax.fori_loop(0, HEADS, query_grads, 0, unroll=HEADS)
     dq_copy = remote(
         dqs.at[other], dq_out.at[:, half], dq_send.at[0], dq_recv.at[0], 2 * chip + other, hd
     )
@@ -267,19 +268,17 @@
             total += inbox[step, which].astype(jnp.float32)
         totals[which] = total.astype(totals.dtype)
     fin_copies = []
-    for which, out in enumerate((dk_out, dv_out)):
-        for k in range(len(PARTNERS)):
-            pcore, ph = partner(k)
-            src_rows = pl.ds(pl.multiple_of(pcore * TOK + PIECE * ph, PIECE), PIECE)
-            copy = remote(
-                totals.at[which, src_rows], out.at[:, mine],
-                fin_send.at[which, k], fin_recv.at[which, k], 2 * chip + pcore, ph,
-            )
-            copy.start()
-            fin_copies.append(copy)
+    for k in range(len(PARTNERS)):
+        pcore, ph = partner(k)
+        src_rows = pl.ds(pl.multiple_of(pcore * TOK + PIECE * ph, PIECE), PIECE)
+        copy = remote(
+            totals.at[:, src_rows], dkv_out.at[:, :, mine],
+            fin_send.at[k], fin_recv.at[k], 2 * chip + pcore, ph,
+        )
+        copy.start()
+        fin_copies.append(copy)
     own_rows = pl.ds(pl.multiple_of(core * TOK + PIECE * hd, PIECE), PIECE)
-    loc_dk = local(7, totals.at[0, own_rows], dk_out.at[:, mine])
-    loc_dv = local(8, totals.at[1, own_rows], dv_out.at[:, mine])
+    loc_dkv = local(8, totals.at[:, own_rows], dkv_out.at[:, :, mine])
 
     for copy in kv_copies + pair_copies:
         copy.wait_send()
@@ -294,10 +293,22 @@
             back[step - 1].wait_send()
 
     loc_dq.wait()
-    loc_dk.wait()
-    loc_dv.wait()
+    loc_dkv.wait()
     dq_copy.wait()
     for copy in fin_copies:
+        copy.wait()
+
+
+def store(dq, dkv, dq_out, dk_out, dv_out, sems):
+    copies = [
+        pltpu.make_async_copy(src, dst, sems.at[k])
+        for k, (src, dst) in enumerate(
+            ((dq, dq_out), (dkv.at[0], dk_out), (dkv.at[1], dv_out))
+        )
+    ]
+    for copy in copies:
+        copy.start()
+    for copy in copies:
         copy.wait()
 
 
@@ -306,22 +317,21 @@
     tokens = query.shape[0]
     dma = pltpu.SemaphoreType.DMA
     partners = len(PARTNERS)
-    return tuple(pl.pallas_call(
+    dq, dkv = pl.pallas_call(
         kernel,
         out_shape=(
             pltpu.VMEM(query.shape, low),
-            pltpu.VMEM(keys.shape, low),
-            pltpu.VMEM(values.shape, low),
+            pltpu.VMEM((2,) + keys.shape, low),
         ),
         in_specs=[pl.BlockSpec(memory_space=pl.ANY)] * 6,
-        out_specs=[pl.BlockSpec(memory_space=pltpu.VMEM)] * 3,
+        out_specs=[pl.BlockSpec(memory_space=pltpu.VMEM)] * 2,
         scratch_shapes=[
+            pltpu.VMEM((2,) + keys.shape, low),
             pltpu.VMEM((PAIR, HALF), low),
             pltpu.VMEM((PAIR, HALF), low),
             pltpu.VMEM((2,) + delta.shape[::-1], full),
             pltpu.VMEM((segments.shape[0] // TOK, TOK), jnp.int32),
-            pltpu.VMEM((SPAN, HD), low),
-            pltpu.VMEM((SPAN, HD), low),
+            pltpu.VMEM((2, SPAN, HD), low),
             pltpu.VMEM((HD, SPAN), low),
             pltpu.VMEM((HEADS, SPAN, PAIR), full),
             pltpu.VMEM((HEADS, SPAN, PAIR), full),
@@ -334,17 +344,24 @@
             pltpu.VMEM((2, PAIR, HD), low),
             pltpu.VMEM((2, tokens, HALF), low),
             dma((9,)),
-            dma((2, partners)), dma((2, partners)),
+            dma((partners,)), dma((partners,)),
             dma((3,)), dma((3,)),
             dma((2, 2)), dma((2, 2)),
             dma((2,)), dma((2,)),
-            dma((2, partners)), dma((2, partners)),
+            dma((partners,)), dma((partners,)),
             dma((1,)), dma((1,)),
         ],
         compiler_params=pltpu.CompilerParams(
             collective_id=0, has_side_effects=True, vmem_limit_bytes=62 * 2**20
         ),
-    )(query, keys, values, grad_out, delta.T, segments.reshape(-1, TOK)))
+    )(query, keys, values, grad_out, delta.T, segments.reshape(-1, TOK))
+    return tuple(pl.pallas_call(
+        store,
+        out_shape=tuple(jax.ShapeDtypeStruct(a.shape, low) for a in (query, keys, values)),
+        in_specs=[pl.BlockSpec(memory_space=pltpu.VMEM)] * 2,
+        out_specs=[pl.BlockSpec(memory_space=pl.ANY)] * 3,
+        scratch_shapes=[dma((3,))],
+    )(*(pltpu.with_memory_space_constraint(a, pltpu.VMEM) for a in (dq, dkv))))
 
 
 def solution(mesh):

time: 42.6 us -> 38.7 us (0.908)
  local copies, waits for them, and re-layouts: 2.05 us -> 0 us
  Pallas kernels: 39.8 us -> 37.9 us
    pallas_call x1, Pallas kernels: 39.8 us -> 37.1 us  [on_device(): pl.pallas_call(kernel, out_shape=(pltpu.VMEM(query.shape, low), pltpu.VME...]
    unnamed x3 -> x0, local copies, waits for them, and re-layouts: 2.05 us -> none
    pallas_call x0 -> x1, Pallas kernels: none -> 0.85 us  [on_device(): pl.pallas_call(store, out_shape=tuple((jax.ShapeDtypeStruct(a.shape, low)...]
where the time goes in v2:
time: 38.7 us; the launch traced here: 38.6 us
  Pallas kernels  37.9 us (98%)
  between operations  0.64 us (2%)
    pallas_call x1, Pallas kernels, on_device(): pl.pallas_call(kernel, out_shape=(pltpu.VMEM(query.shape, low), pltpu.VME...  37.1 us
    pallas_call x1, Pallas kernels, on_device(): pl.pallas_call(store, out_shape=tuple((jax.ShapeDtypeStruct(a.shape, low)...  0.85 us

profile of v2, /device:TPU:231, one launch (start us, length us, event | category | flops | bytes accessed | tf_op | source)
XLA Modules:
  0.0 38.6 jit_solution(2371272761118688529)
XLA Ops:
  0.6 37.1 %shard_map.85 = (bf16[128,2048]{1,0:T(8,128)(2,1)S(1)}, bf16[2,32,1024]{2,1,0:T(8,128)(2,1)S(1)}) custom-call(bf16[128,2048]{1,0:T(8,128)(2,1)} %query.1, bf16[32,1024]{1,0:T(8,128)(2,1)} %keys.1, bf16[32,1024]{1,0:T(8,128)(2,1)} %values.1, bf16[128,2048]{1,0:T(8,128)(2,1)} %grad_out.1, f32[16,128]{1,0:T(8,128)} %bitcast.3, s32[128,128]{1,0:T(8,128)} %bitcast.2), custom_call_target="tpu_custom_call" | custom-call | tf_op jit(solution)/shard_map/pallas_call | solution.py:320
  37.7 0.9 %shard_map.86 = (bf16[128,2048]{1,0:T(8,128)(2,1)}, bf16[32,1024]{1,0:T(8,128)(2,1)}, bf16[32,1024]{1,0:T(8,128)(2,1)}) custom-call(bf16[128,2048]{1,0:T(8,128)(2,1)S(1)} %get-tuple-element.5.dq, bf16[2,32,1024]{2,1,0:T(8,128)(2,1)S(1)} %get-tuple-element.6.dkv), custom_call_target="tpu_custom_call" | custom-call | tf_op jit(solution)/shard_map/pallas_call | solution.py:358

commit v3 on v2

--- a/solution.py
+++ b/solution.py
@@ -86,17 +86,19 @@
 
     for copy in loc_stage:
         copy.wait()
-    kv_copies = []
-    for k in range(len(PARTNERS)):
-        pcore, ph = partner(k)
-        cols = pl.ds(aligned(2 * ph + pcore, HD), HD)
-        copy = remote(
-            stage.at[:, :, cols], kv.at[:, slot],
-            kv_send.at[k], kv_recv.at[k], 2 * chip + pcore, ph,
-        )
-        copy.start()
-        kv_copies.append(copy)
-    loc_kv = local(7, stage.at[:, :, mine], kv.at[:, slot])
+    kv_copies = [[], []]
+    loc_kv = []
+    for which in range(2):
+        for k in range(len(PARTNERS)):
+            pcore, ph = partner(k)
+            cols = pl.ds(aligned(2 * ph + pcore, HD), HD)
+            copy = remote(
+                stage.at[which, :, cols], kv.at[which, slot],
+                kv_send.at[which, k], kv_recv.at[which, k], 2 * chip + pcore, ph,
+            )
+            copy.start()
+            kv_copies[which].append(copy)
+        loc_kv.append(local(7 + which, stage.at[which, :, mine], kv.at[which, slot]))
     pair_copies = []
     for k, (src, dst) in enumerate((
         (query.at[:, far_half], qb.at[my_rows]),
@@ -143,11 +145,11 @@
             ref[SEEN:SPAN, head * PAIR : head * PAIR + TOK] = nothing
             ref[0:TOK, head * PAIR + TOK : (head + 1) * PAIR] = nothing
 
-    shift = [[[None] * 2 for _ in range(2)] for _ in range(2)]
-    loc_kv.wait()
-    for copy in kv_copies:
-        copy.wait_recv()
+    shift = [[None] * 2, [None] * 2]
     for which in range(2):
+        loc_kv[which].wait()
+        for copy in kv_copies[which]:
+            copy.wait_recv()
         for step in (2, 1):
             copy = remote(
                 kv.at[which, pl.ds(2 * PAIR, PAIR)],
@@ -155,7 +157,7 @@
                 shift_send.at[step - 1, which], shift_recv.at[step - 1, which],
                 tok + 2 * step, hd,
             )
-            shift[step - 1][which] = copy
+            shift[which][step - 1] = copy
 
             @pl.when(chip + step < chips)
             def _(copy=copy):
@@ -167,80 +169,101 @@
     for copy in pair_copies:
         copy.wait_recv()
 
-    def products(block):
+    def over_heads(body):
+        def step(head, _):
+            body(head)
+            return 0
+
+        lax.fori_loop(0, HEADS, step, 0, unroll=HEADS)
+
+    def products(which, block):
         span = slice(block * PAIR, (block + 1) * PAIR)
-
-        def body(head, _):
+        rows_of, result = ((qb, scores), (gb, gweights))[which]
+
+        def body(head):
             cols = pl.ds(aligned(head, HD), HD)
-            scores[head, span, :] = lax.dot_general(
-                kv[0, span, :], qb[:, cols], NT, preferred_element_type=jnp.float32
-            )
-            gweights[head, span, :] = lax.dot_general(
-                kv[1, span, :], gb[:, cols], NT, preferred_element_type=jnp.float32
-            )
-            return 0
-
-        lax.fori_loop(0, HEADS, body, 0, unroll=HEADS)
-        kt[:, span] = jnp.transpose(kv[0, span, :])
-
-    products(2)
-    for step in (1, 2):
+            result[head, span, :] = lax.dot_general(
+                kv[which, span, :], rows_of[:, cols], NT, preferred_element_type=jnp.float32
+            )
+
+        over_heads(body)
+
+    def arrival(which, step):
         @pl.when(chip >= step)
-        def _(step=step):
-            for which in range(2):
-                shift[step - 1][which].wait_recv()
-
-        products(2 - step)
-
-    def softmax(head, _):
+        def _():
+            shift[which][step - 1].wait_recv()
+
+    def parts(head, b):
+        span = slice(b * TOK, b * TOK + SEEN)
+        lanes = slice(b * TOK, (b + 1) * TOK)
+        cols = pl.ds(pl.multiple_of(head * PAIR + b * TOK, TOK), TOK)
+        return span, lanes, cols
+
+    def softmax(head):
         for b in range(2):
-            span = slice(b * TOK, b * TOK + SEEN)
-            lanes = slice(b * TOK, (b + 1) * TOK)
+            span, lanes, cols = parts(head, b)
             raw = scores[head, span, lanes] + bias[b]
             top = jnp.max(raw, axis=0, keepdims=True)
             grown = jnp.exp2((raw - top) * (SCALE * LOG2E))
             total = jnp.sum(grown, axis=0, keepdims=True)
             weights = grown * (1.0 / total)
+            scores[head, span, lanes] = weights
+            probs[span, cols] = weights.astype(probs.dtype)
+
+    def score_grads(head):
+        for b in range(2):
+            span, lanes, cols = parts(head, b)
             row_delta = dt[b, pl.ds(core * HEADS + head, 1), :]
-            grads = weights * (gweights[head, span, lanes] - row_delta)
-            cols = pl.ds(pl.multiple_of(head * PAIR + b * TOK, TOK), TOK)
-            probs[span, cols] = weights.astype(probs.dtype)
+            grads = scores[head, span, lanes] * (gweights[head, span, lanes] - row_delta)
             dscores[span, cols] = grads.astype(dscores.dtype)
-        return 0
-
-    lax.fori_loop(0, HEADS, softmax, 0, unroll=HEADS)
-
-    def key_value_grads(block):
+
+    def grads_of(which, block):
         span = slice(block * PAIR, (block + 1) * PAIR)
-        dk = jnp.zeros((PAIR, HD), jnp.float32)
-        dv = jnp.zeros((PAIR, HD), jnp.float32)
+        terms, rows_of = ((dscores, qb), (probs, gb))[which]
+        total = jnp.zeros((PAIR, HD), jnp.float32)
         for head in range(HEADS):
-            lanes = slice(head * PAIR, (head + 1) * PAIR)
-            cols = slice(head * HD, (head + 1) * HD)
-            dk += jnp.dot(dscores[span, lanes], qb[:, cols], preferred_element_type=jnp.float32)
-            dv += jnp.dot(probs[span, lanes], gb[:, cols], preferred_element_type=jnp.float32)
-        return dk * SCALE, dv
-
-    back = [None, None]
-    for step in (2, 1):
-        dk, dv = key_value_grads(2 - step)
-        outbox[step - 1, 0] = dk.astype(outbox.dtype)
-        outbox[step - 1, 1] = dv.astype(outbox.dtype)
-        copy = remote(
-            outbox.at[step - 1], inbox.at[step - 1],
-            back_send.at[step - 1], back_recv.at[step - 1], tok - 2 * step, hd,
-        )
-        back[step - 1] = copy
-
-        @pl.when(chip >= step)
-        def _(copy=copy):
-            copy.start()
-
-    dk, dv = key_value_grads(2)
-    own[0] = dk
-    own[1] = dv
-
-    def query_grads(head, _):
+            total += jnp.dot(
+                terms[span, head * PAIR : (head + 1) * PAIR],
+                rows_of[:, head * HD : (head + 1) * HD],
+                preferred_element_type=jnp.float32,
+            )
+        return total if which else total * SCALE
+
+    def send_back(which):
+        for step in (2, 1):
+            outbox[step - 1, which] = grads_of(which, 2 - step).astype(outbox.dtype)
+            copy = remote(
+                outbox.at[step - 1, which], inbox.at[step - 1, which],
+                back_send.at[step - 1, which], back_recv.at[step - 1, which],
+                tok - 2 * step, hd,
+            )
+            back[which][step - 1] = copy
+
+            @pl.when(chip >= step)
+            def _(copy=copy):
+                copy.start()
+
+        own[which] = grads_of(which, 2)
+
+    back = [[None] * 2, [None] * 2]
+    products(0, 2)
+    products(1, 2)
+    for step in (1, 2):
+        arrival(0, step)
+        products(0, 2 - step)
+    over_heads(softmax)
+    send_back(1)
+    for step in (1, 2):
+        arrival(1, step)
+        products(1, 2 - step)
+    over_heads(score_grads)
+    send_back(0)
+
+    for block in range(3):
+        span = slice(block * PAIR, (block + 1) * PAIR)
+        kt[:, span] = jnp.transpose(kv[0, span, :])
+
+    def query_grads(head):
         lanes = pl.ds(aligned(head, PAIR), PAIR)
         turned = jnp.dot(kt[...], dscores[:, lanes], preferred_element_type=jnp.float32)
         turned = turned * SCALE
@@ -248,52 +271,54 @@
         for b in range(2):
             block = jnp.transpose(turned[:, b * TOK : (b + 1) * TOK])
             dqs[b, :, cols] = block.astype(dqs.dtype)
-        return 0
-
-    lax.fori_loop(0, HEADS, query_grads, 0, unroll=HEADS)
+
+    over_heads(query_grads)
     dq_copy = remote(
         dqs.at[other], dq_out.at[:, half], dq_send.at[0], dq_recv.at[0], 2 * chip + other, hd
     )
     dq_copy.start()
     loc_dq = local(6, dqs.at[core], dq_out.at[:, half])
 
-    for step in (1, 2):
-        @pl.when(chip + step < chips)
-        def _(step=step):
-            back[step - 1].wait_recv()
-
-    for which in range(2):
+    own_rows = pl.ds(pl.multiple_of(core * TOK + PIECE * hd, PIECE), PIECE)
+    fin_copies = []
+    loc_out = []
+    for which in (1, 0):
+        for step in (1, 2):
+            @pl.when(chip + step < chips)
+            def _(step=step, which=which):
+                back[which][step - 1].wait_recv()
+
         total = own[which]
         for step in range(2):
             total += inbox[step, which].astype(jnp.float32)
         totals[which] = total.astype(totals.dtype)
-    fin_copies = []
-    for k in range(len(PARTNERS)):
-        pcore, ph = partner(k)
-        src_rows = pl.ds(pl.multiple_of(pcore * TOK + PIECE * ph, PIECE), PIECE)
-        copy = remote(
-            totals.at[:, src_rows], dkv_out.at[:, :, mine],
-            fin_send.at[k], fin_recv.at[k], 2 * chip + pcore, ph,
-        )
-        copy.start()
-        fin_copies.append(copy)
-    own_rows = pl.ds(pl.multiple_of(core * TOK + PIECE * hd, PIECE), PIECE)
-    loc_dkv = local(8, totals.at[:, own_rows], dkv_out.at[:, :, mine])
-
-    for copy in kv_copies + pair_copies:
+        for k in range(len(PARTNERS)):
+            pcore, ph = partner(k)
+            src_rows = pl.ds(pl.multiple_of(pcore * TOK + PIECE * ph, PIECE), PIECE)
+            copy = remote(
+                totals.at[which, src_rows], dkv_out.at[which, :, mine],
+                fin_send.at[which, k], fin_recv.at[which, k], 2 * chip + pcore, ph,
+            )
+            copy.start()
+            fin_copies.append(copy)
+        loc_out.append(local(9 + which, totals.at[which, own_rows], dkv_out.at[which, :, mine]))
+
+    for copy in kv_copies[0] + kv_copies[1] + pair_copies:
         copy.wait_send()
     for step in (1, 2):
         @pl.when(chip + step < chips)
         def _(step=step):
             for which in range(2):
-                shift[step - 1][which].wait_send()
+                shift[which][step - 1].wait_send()
 
         @pl.when(chip >= step)
         def _(step=step):
-            back[step - 1].wait_send()
+            for which in range(2):
+                back[which][step - 1].wait_send()
 
     loc_dq.wait()
-    loc_dkv.wait()
+    for copy in loc_out:
+        copy.wait()
     dq_copy.wait()
     for copy in fin_copies:
         copy.wait()
@@ -343,12 +368,12 @@
             pltpu.VMEM((2, 2, PAIR, HD), low),
             pltpu.VMEM((2, PAIR, HD), low),
             pltpu.VMEM((2, tokens, HALF), low),
-            dma((9,)),
-            dma((partners,)), dma((partners,)),
+            dma((11,)),
+            dma((2, partners)), dma((2, partners)),
             dma((3,)), dma((3,)),
             dma((2, 2)), dma((2, 2)),
-            dma((2,)), dma((2,)),
-            dma((partners,)), dma((partners,)),
+            dma((2, 2)), dma((2, 2)),
+            dma((2, partners)), dma((2, partners)),
             dma((1,)), dma((1,)),
         ],
         compiler_params=pltpu.CompilerParams(

time: 38.7 us -> 34.9 us (0.902)
  Pallas kernels: 37.9 us -> 34.1 us
    pallas_call x1, Pallas kernels: 37.1 us -> 33.3 us  [on_device(): pl.pallas_call(kernel, out_shape=(pltpu.VMEM(query.shape, low), pltpu.VME...]
where the time goes in v3:
time: 34.9 us; the launch traced here: 34.8 us
  Pallas kernels  34.1 us (98%)
  between operations  0.64 us (2%)
    pallas_call x1, Pallas kernels, on_device(): pl.pallas_call(kernel, out_shape=(pltpu.VMEM(query.shape, low), pltpu.VME...  33.3 us
    pallas_call x1, Pallas kernels, on_device(): pl.pallas_call(store, out_shape=tuple((jax.ShapeDtypeStruct(a.shape, low)...  0.85 us

profile of v3, /device:TPU:231, one launch (start us, length us, event | category | flops | bytes accessed | tf_op | source)
XLA Modules:
  0.0 34.8 jit_solution(16886388196226348786)
XLA Ops:
  0.6 33.3 %shard_map.85 = (bf16[128,2048]{1,0:T(8,128)(2,1)S(1)}, bf16[2,32,1024]{2,1,0:T(8,128)(2,1)S(1)}) custom-call(bf16[128,2048]{1,0:T(8,128)(2,1)} %query.1, bf16[32,1024]{1,0:T(8,128)(2,1)} %keys.1, bf16[32,1024]{1,0:T(8,128)(2,1)} %values.1, bf16[128,2048]{1,0:T(8,128)(2,1)} %grad_out.1, f32[16,128]{1,0:T(8,128)} %bitcast.3, s32[128,128]{1,0:T(8,128)} %bitcast.2), custom_call_target="tpu_custom_call" | custom-call | tf_op jit(solution)/shard_map/pallas_call | solution.py:345
  33.9 0.9 %shard_map.86 = (bf16[128,2048]{1,0:T(8,128)(2,1)}, bf16[32,1024]{1,0:T(8,128)(2,1)}, bf16[32,1024]{1,0:T(8,128)(2,1)}) custom-call(bf16[128,2048]{1,0:T(8,128)(2,1)S(1)} %get-tuple-element.5.dq, bf16[2,32,1024]{2,1,0:T(8,128)(2,1)S(1)} %get-tuple-element.6.dkv), custom_call_target="tpu_custom_call" | custom-call | tf_op jit(solution)/shard_map/pallas_call | solution.py:383

commit v4 on v3

v4 whole, which is shorter than its diff:
```python
import math

import jax
import jax.numpy as jnp
from jax import lax
from jax.experimental import pallas as pl
from jax.experimental.pallas import tpu as pltpu
from jax.sharding import PartitionSpec as P

MESH = pl.DeviceIdType.MESH
HD = 128
HEADS = 8
TOK = 128
PAIR = 2 * TOK
SPAN = 3 * PAIR
SEEN = 5 * TOK
HALF = HEADS * HD
PIECE = 32
FILL = -1e30
SCALE = 1.0 / math.sqrt(HD)
LOG2E = math.log2(math.e)
PLACES = [(0, 2), (1, 2), (0, 1), (0, 3), (1, 1), (1, 3), (1, 0), (0, 0)]
STEPS = (2, 1, 0)
NT = (((1,), (1,)), ((), ()))


def aligned(index, size):
    return pl.multiple_of(index * size, size)


def kernel(
    query, keys, values, grad_out, delta, segments,
    dq_out, dkv_out,
    stage, qb, gb, dt, sb, kv, kt, scores, gweights, probs, dscores, bias, stats,
    terms, gathered, dqs,
    local_sem, kv_send, kv_recv, pair_send, pair_recv,
    back_send, back_recv, dq_send, dq_recv,
):
    tok, hd = lax.axis_index("tok"), lax.axis_index("hd")
    chips = lax.axis_size("tok") // 2
    rows_y = lax.axis_size("hd")
    core, chip = lax.rem(tok, 2), lax.div(tok, 2)
    other = 1 - core

    def local(index, src, dst):
        copy = pltpu.make_async_copy(src, dst, local_sem.at[index])
        copy.start()
        return copy

    def remote(src, dst, send, recv, to_tok, to_hd):
        return pltpu.make_async_remote_copy(
            src_ref=src, dst_ref=dst, send_sem=send, recv_sem=recv,
            device_id=(to_tok, to_hd), device_id_type=MESH,
        )

    def place(k):
        cross, step = PLACES[k]
        pcore = other if cross else core
        return pcore, lax.rem(hd + step, rows_y)

    def places(step):
        return range(len(PLACES) if step else len(PLACES) - 1)

    def only_if(step, condition, action):
        if step:
            pl.when(condition)(action)
        else:
            action()

    mine = pl.ds(aligned(2 * hd + core, HD), HD)
    half = pl.ds(aligned(core, HALF), HALF)
    far_half = pl.ds(aligned(other, HALF), HALF)
    my_rows = pl.ds(aligned(core, TOK), TOK)
    loc_stage = [local(0, keys, stage.at[0]), local(1, values, stage.at[1])]
    loc_s = local(2, segments, sb)

    barrier = pltpu.get_barrier_semaphore()
    for step in STEPS:
        for ahead in (1, -1) if step else (1,):
            def greet(step=step, ahead=ahead):
                for k in places(step):
                    pcore, ph = place(k)
                    pl.semaphore_signal(
                        barrier, 1, device_id=(2 * (chip + ahead * step) + pcore, ph),
                        device_id_type=MESH,
                    )

            only_if(step, chip + step < chips if ahead > 0 else chip >= step, greet)

    near = sum(
        jnp.where(c, 1, 0)
        for c in (chip >= 1, chip >= 2, chip + 1 < chips, chip + 2 < chips)
    )
    pl.semaphore_wait(barrier, len(PLACES) - 1 + len(PLACES) * near)

    for copy in loc_stage:
        copy.wait()
    kv_copies = [[[] for _ in range(3)] for _ in range(2)]
    loc_kv = []

    def send_rows(which):
        for step in STEPS:
            slot = pl.ds(
                pl.multiple_of((4 - 2 * step + core) * TOK + PIECE * hd, PIECE), PIECE
            )
            for k in places(step):
                pcore, ph = place(k)
                cols = pl.ds(aligned(2 * ph + pcore, HD), HD)
                kv_copies[which][step].append(remote(
                    stage.at[which, :, cols], kv.at[which, slot],
                    kv_send.at[which, step, k], kv_recv.at[which, step, k],
                    2 * (chip + step) + pcore, ph,
                ))

            def start(step=step):
                for copy in kv_copies[which][step]:
                    copy.start()

            only_if(step, chip + step < chips, start)
        loc_kv.append(local(7 + which, stage.at[which, :, mine], kv.at[which, slot]))

    pair_copies = []

    def to_other_core(src, dst):
        k = len(pair_copies)
        copy = remote(src, dst, pair_send.at[k], pair_recv.at[k], 2 * chip + other, hd)
        copy.start()
        pair_copies.append(copy)

    send_rows(0)
    to_other_core(query.at[:, far_half], qb.at[my_rows])
    loc_q = local(3, query.at[:, half], qb.at[my_rows])
    send_rows(1)
    to_other_core(grad_out.at[:, far_half], gb.at[my_rows])
    to_other_core(delta, dt.at[core])
    loc_g = local(4, grad_out.at[:, half], gb.at[my_rows])
    loc_d = local(5, delta, dt.at[core])

    for step in (1, 2):
        @pl.when(chip < step)
        def _(step=step):
            empty = pl.ds((2 - step) * PAIR, PAIR)
            kv[:, empty, :] = jnp.zeros((2, PAIR, HD), kv.dtype)

        @pl.when(chip + step >= chips)
        def _(step=step):
            for which in range(2):
                gathered[which, step] = jnp.zeros(gathered.shape[2:], gathered.dtype)

    loc_s.wait()

    def ids(shard):
        row = sb[pl.ds(jnp.maximum(shard, 0), 1), :]
        return jnp.where(shard < 0, -1, row)

    shards = [2 * chip - 4 + s for s in range(6)]
    rows = [ids(s) for s in shards]
    tall = [jnp.transpose(jnp.broadcast_to(r, (TOK, TOK))) for r in rows]
    key_at = lax.broadcasted_iota(jnp.int32, (TOK, TOK), 0)
    query_at = lax.broadcasted_iota(jnp.int32, (TOK, TOK), 1)
    for b in range(2):
        for s in range(5):
            allowed = tall[b + s] == rows[4 + b]
            if s == 4:
                allowed = allowed & (key_at <= query_at)
            bias[b, s * TOK : (s + 1) * TOK, :] = jnp.where(allowed, 0.0, FILL)
    nothing = jnp.zeros((TOK, TOK), probs.dtype)
    for head in range(HEADS):
        for ref in (probs, dscores):
            ref[SEEN:SPAN, head * PAIR : head * PAIR + TOK] = nothing
            ref[0:TOK, head * PAIR + TOK : (head + 1) * PAIR] = nothing

    loc_q.wait()
    loc_g.wait()
    loc_d.wait()
    for copy in pair_copies:
        copy.wait_recv()

    def over_heads(body):
        def step(head, _):
            body(head)
            return 0

        lax.fori_loop(0, HEADS, step, 0, unroll=HEADS)

    def products(which, block):
        span = slice(block * PAIR, (block + 1) * PAIR)
        rows_of, result = ((qb, scores), (gb, gweights))[which]

        def body(head):
            cols = pl.ds(aligned(head, HD), HD)
            result[head, span, :] = lax.dot_general(
                kv[which, span, :], rows_of[:, cols], NT, preferred_element_type=jnp.float32
            )

        over_heads(body)

    def arrival(which, step):
        def wait():
            for copy in kv_copies[which][step]:
                copy.wait_recv()
            if not step:
                loc_kv[which].wait()

        only_if(step, chip >= step, wait)

    def lanes_of(head, b):
        lanes = slice(b * TOK, (b + 1) * TOK)
        cols = pl.ds(pl.multiple_of(head * PAIR + b * TOK, TOK), TOK)
        return lanes, cols

    def near_part(head):
        for b in range(2):
            span = slice(PAIR, b * TOK + SEEN)
            lanes, _ = lanes_of(head, b)
            raw = scores[head, span, lanes] + bias[b, PAIR - b * TOK : SEEN, :]
            top = jnp.max(raw, axis=0, keepdims=True)
            grown = jnp.exp2((raw - top) * (SCALE * LOG2E))
            scores[head, span, lanes] = grown
            stats[0, b, pl.ds(head, 1), :] = top
            stats[1, b, pl.ds(head, 1), :] = jnp.sum(grown, axis=0, keepdims=True)

    def far_part(head):
        for b in range(2):
            span = slice(b * TOK, PAIR)
            lanes, cols = lanes_of(head, b)
            raw = scores[head, span, lanes] + bias[b, 0 : PAIR - b * TOK, :]
            near_top = stats[0, b, pl.ds(head, 1), :]
            near_total = stats[1, b, pl.ds(head, 1), :]
            top = jnp.maximum(near_top, jnp.max(raw, axis=0, keepdims=True))
            grown = jnp.exp2((raw - top) * (SCALE * LOG2E))
            lift = jnp.exp2((near_top - top) * (SCALE * LOG2E))
            total = near_total * lift + jnp.sum(grown, axis=0, keepdims=True)
            share = 1.0 / total
            weights = grown * share
            stats[0, b, pl.ds(head, 1), :] = lift * share
            scores[head, span, lanes] = weights
            probs[span, cols] = weights.astype(probs.dtype)

    def near_weights(head):
        for b in range(2):
            span = slice(PAIR, b * TOK + SEEN)
            lanes, cols = lanes_of(head, b)
            weights = scores[head, span, lanes] * stats[0, b, pl.ds(head, 1), :]
            scores[head, span, lanes] = weights
            probs[span, cols] = weights.astype(probs.dtype)

    def score_grads(head):
        for b in range(2):
            span = slice(b * TOK, b * TOK + SEEN)
            lanes, cols = lanes_of(head, b)
            row_delta = dt[b, pl.ds(core * HEADS + head, 1), :]
            grads = scores[head, span, lanes] * (gweights[head, span, lanes] - row_delta)
            dscores[span, cols] = grads.astype(dscores.dtype)

    def grads_of(which, block):
        span = slice(block * PAIR, (block + 1) * PAIR)
        factors, rows_of = ((dscores, qb), (probs, gb))[which]
        total = jnp.zeros((PAIR, HD), jnp.float32)
        for head in range(HEADS):
            total += jnp.dot(
                factors[span, head * PAIR : (head + 1) * PAIR],
                rows_of[:, head * HD : (head + 1) * HD],
                preferred_element_type=jnp.float32,
            )
        return total if which else total * SCALE

    def rows_at(k):
        pcore, ph = place(k)
        return pl.ds(pl.multiple_of(pcore * TOK + PIECE * ph, PIECE), PIECE)

    back = [[[] for _ in range(3)] for _ in range(2)]
    loc_back = [None] * 2

    def send_back(which, step):
        terms[which, step] = grads_of(which, 2 - step).astype(terms.dtype)
        for k in places(step):
            pcore, ph = place(k)
            back[which][step].append(remote(
                terms.at[which, step, rows_at(k)], gathered.at[which, step, :, mine],
                back_send.at[which, step, k], back_recv.at[which, step, k],
                2 * (chip - step) + pcore, ph,
            ))

        def start():
            for copy in back[which][step]:
                copy.start()

        only_if(step, chip >= step, start)
        if not step:
            own_rows = rows_at(len(PLACES) - 1)
            loc_back[which] = local(
                9 + which, terms.at[which, 0, own_rows], gathered.at[which, 0, :, mine]
            )

    arrival(0, 0)
    products(0, 2)
    arrival(1, 0)
    products(1, 2)
    arrival(0, 1)
    products(0, 1)
    over_heads(near_part)
    arrival(0, 2)
    products(0, 0)
    over_heads(far_part)
    send_back(1, 2)
    over_heads(near_weights)
    send_back(1, 1)
    send_back(1, 0)
    for step in (1, 2):
        arrival(1, step)
        products(1, 2 - step)
    over_heads(score_grads)
    send_back(0, 2)
    send_back(0, 1)
    send_back(0, 0)

    for block in range(3):
        span = slice(block * PAIR, (block + 1) * PAIR)
        kt[:, span] = jnp.transpose(kv[0, span, :])

    def query_grads(head):
        lanes = pl.ds(aligned(head, PAIR), PAIR)
        turned = jnp.dot(kt[...], dscores[:, lanes], preferred_element_type=jnp.float32)
        turned = turned * SCALE
        cols = pl.ds(aligned(head, HD), HD)
        for b in range(2):
            block = jnp.transpose(turned[:, b * TOK : (b + 1) * TOK])
            dqs[b, :, cols] = block.astype(dqs.dtype)

    over_heads(query_grads)
    dq_copy = remote(
        dqs.at[other], dq_out.at[:, half], dq_send.at[0], dq_recv.at[0], 2 * chip + other, hd
    )
    dq_copy.start()
    loc_dq = local(6, dqs.at[core], dq_out.at[:, half])

    for which in (1, 0):
        for step in STEPS:
            def wait(which=which, step=step):
                for copy in back[which][step]:
                    copy.wait_recv()

            only_if(step, chip + step < chips, wait)
        loc_back[which].wait()
        total = gathered[which, 0].astype(jnp.float32)
        for step in (1, 2):
            total += gathered[which, step].astype(jnp.float32)
        dkv_out[which] = total.astype(dkv_out.dtype)

    for copy in pair_copies:
        copy.wait_send()
    for which in range(2):
        for step in STEPS:
            def sent(copies):
                for copy in copies:
                    copy.wait_send()

            only_if(step, chip + step < chips, lambda: sent(kv_copies[which][step]))
            only_if(step, chip >= step, lambda: sent(back[which][step]))
    loc_dq.wait()
    dq_copy.wait()


def store(dq, dkv, dq_out, dk_out, dv_out, sems):
    copies = [
        pltpu.make_async_copy(src, dst, sems.at[k])
        for k, (src, dst) in enumerate(
            ((dq, dq_out), (dkv.at[0], dk_out), (dkv.at[1], dv_out))
        )
    ]
    for copy in copies:
        copy.start()
    for copy in copies:
        copy.wait()


def on_device(query, keys, values, grad_out, delta, segments):
    low, full = jnp.bfloat16, jnp.float32
    tokens = query.shape[0]
    dma = pltpu.SemaphoreType.DMA
    places = len(PLACES)
    dq, dkv = pl.pallas_call(
        kernel,
        out_shape=(
            pltpu.VMEM(query.shape, low),
            pltpu.VMEM((2,) + keys.shape, low),
        ),
        in_specs=[pl.BlockSpec(memory_space=pl.ANY)] * 6,
        out_specs=[pl.BlockSpec(memory_space=pltpu.VMEM)] * 2,
        scratch_shapes=[
            pltpu.VMEM((2,) + keys.shape, low),
            pltpu.VMEM((PAIR, HALF), low),
            pltpu.VMEM((PAIR, HALF), low),
            pltpu.VMEM((2,) + delta.shape[::-1], full),
            pltpu.VMEM((segments.shape[0] // TOK, TOK), jnp.int32),
            pltpu.VMEM((2, SPAN, HD), low),
            pltpu.VMEM((HD, SPAN), low),
            pltpu.VMEM((HEADS, SPAN, PAIR), full),
            pltpu.VMEM((HEADS, SPAN, PAIR), full),
            pltpu.VMEM((SPAN, HEADS * PAIR), low),
            pltpu.VMEM((SPAN, HEADS * PAIR), low),
            pltpu.VMEM((2, SEEN, TOK), full),
            pltpu.VMEM((2, 2, HEADS, TOK), full),
            pltpu.VMEM((2, 3, PAIR, HD), low),
            pltpu.VMEM((2, 3) + keys.shape, low),
            pltpu.VMEM((2, tokens, HALF), low),
            dma((11,)),
            dma((2, 3, places)), dma((2, 3, places)),
            dma((3,)), dma((3,)),
            dma((2, 3, places)), dma((2, 3, places)),
            dma((1,)), dma((1,)),
        ],
        compiler_params=pltpu.CompilerParams(
            collective_id=0, has_side_effects=True, vmem_limit_bytes=62 * 2**20
        ),
    )(query, keys, values, grad_out, delta.T, segments.reshape(-1, TOK))
    return tuple(pl.pallas_call(
        store,
        out_shape=tuple(jax.ShapeDtypeStruct(a.shape, low) for a in (query, keys, values)),
        in_specs=[pl.BlockSpec(memory_space=pltpu.VMEM)] * 2,
        out_specs=[pl.BlockSpec(memory_space=pl.ANY)] * 3,
        scratch_shapes=[dma((3,))],
    )(*(pltpu.with_memory_space_constraint(a, pltpu.VMEM) for a in (dq, dkv))))


def solution(mesh):
    return jax.shard_map(
        on_device,
        mesh=mesh,
        in_specs=(
            P("tok", "hd"),
            P(("tok", "hd"), None),
            P(("tok", "hd"), None),
            P("tok", "hd"),
            P("tok", "hd"),
            P(),
        ),
        out_specs=(P("tok", "hd"), P(("tok", "hd"), None), P(("tok", "hd"), None)),
        check_vma=False,
    )
```

time: 34.9 us -> 32.4 us (0.928)
  Pallas kernels: 34.1 us -> 31.6 us
    pallas_call x1, Pallas kernels: 33.3 us -> 30.8 us  [on_device(): pl.pallas_call(kernel, out_shape=(pltpu.VMEM(query.shape, low), pltpu.VME...]
where the time goes in v4:
time: 32.4 us; the launch traced here: 32.3 us
  Pallas kernels  31.6 us (98%)
  between operations  0.64 us (2%)
    pallas_call x1, Pallas kernels, on_device(): pl.pallas_call(kernel, out_shape=(pltpu.VMEM(query.shape, low), pltpu.VME...  30.8 us
    pallas_call x1, Pallas kernels, on_device(): pl.pallas_call(store, out_shape=tuple((jax.ShapeDtypeStruct(a.shape, low)...  0.85 us

profile of v4, /device:TPU:231, one launch (start us, length us, event | category | flops | bytes accessed | tf_op | source)
XLA Modules:
  0.0 32.3 jit_solution(14287830199436864059)
XLA Ops:
  0.6 30.8 %shard_map.85 = (bf16[128,2048]{1,0:T(8,128)(2,1)S(1)}, bf16[2,32,1024]{2,1,0:T(8,128)(2,1)S(1)}) custom-call(bf16[128,2048]{1,0:T(8,128)(2,1)} %query.1, bf16[32,1024]{1,0:T(8,128)(2,1)} %keys.1, bf16[32,1024]{1,0:T(8,128)(2,1)} %values.1, bf16[128,2048]{1,0:T(8,128)(2,1)} %grad_out.1, f32[16,128]{1,0:T(8,128)} %bitcast.3, s32[128,128]{1,0:T(8,128)} %bitcast.2), custom_call_target="tpu_custom_call" | custom-call | tf_op jit(solution)/shard_map/pallas_call | solution.py:383
  31.4 0.9 %shard_map.86 = (bf16[128,2048]{1,0:T(8,128)(2,1)}, bf16[32,1024]{1,0:T(8,128)(2,1)}, bf16[32,1024]{1,0:T(8,128)(2,1)}) custom-call(bf16[128,2048]{1,0:T(8,128)(2,1)S(1)} %get-tuple-element.5.dq, bf16[2,32,1024]{2,1,0:T(8,128)(2,1)S(1)} %get-tuple-element.6.dkv), custom_call_target="tpu_custom_call" | custom-call | tf_op jit(solution)/shard_map/pallas_call | solution.py:418

commit v5 on v4

--- a/solution.py
+++ b/solution.py
@@ -76,21 +76,17 @@
 
     barrier = pltpu.get_barrier_semaphore()
     for step in STEPS:
-        for ahead in (1, -1) if step else (1,):
-            def greet(step=step, ahead=ahead):
-                for k in places(step):
-                    pcore, ph = place(k)
-                    pl.semaphore_signal(
-                        barrier, 1, device_id=(2 * (chip + ahead * step) + pcore, ph),
-                        device_id_type=MESH,
-                    )
-
-            only_if(step, chip + step < chips if ahead > 0 else chip >= step, greet)
-
-    near = sum(
-        jnp.where(c, 1, 0)
-        for c in (chip >= 1, chip >= 2, chip + 1 < chips, chip + 2 < chips)
-    )
+        def greet(step=step):
+            for k in places(step):
+                pcore, ph = place(k)
+                pl.semaphore_signal(
+                    barrier, 1, device_id=(2 * (chip - step) + pcore, ph),
+                    device_id_type=MESH,
+                )
+
+        only_if(step, chip >= step, greet)
+
+    near = sum(jnp.where(c, 1, 0) for c in (chip + 1 < chips, chip + 2 < chips))
     pl.semaphore_wait(barrier, len(PLACES) - 1 + len(PLACES) * near)
 
     for copy in loc_stage:
@@ -245,9 +241,9 @@
             scores[head, span, lanes] = weights
             probs[span, cols] = weights.astype(probs.dtype)
 
-    def score_grads(head):
+    def score_grads(head, far):
         for b in range(2):
-            span = slice(b * TOK, b * TOK + SEEN)
+            span = slice(b * TOK, PAIR) if far else slice(PAIR, b * TOK + SEEN)
             lanes, cols = lanes_of(head, b)
             row_delta = dt[b, pl.ds(core * HEADS + head, 1), :]
             grads = scores[head, span, lanes] * (gweights[head, span, lanes] - row_delta)
@@ -306,13 +302,12 @@
     send_back(1, 2)
     over_heads(near_weights)
     send_back(1, 1)
-    send_back(1, 0)
-    for step in (1, 2):
+    for step in (2, 1):
         arrival(1, step)
         products(1, 2 - step)
-    over_heads(score_grads)
-    send_back(0, 2)
-    send_back(0, 1)
+        over_heads(lambda head: score_grads(head, step == 2))
+        send_back(0, step)
+    send_back(1, 0)
     send_back(0, 0)
 
     for block in range(3):

time: 32.4 us -> 31.7 us (0.978)
  Pallas kernels: 31.6 us -> 30.9 us
    pallas_call x1, Pallas kernels: 30.8 us -> 30 us  [on_device(): pl.pallas_call(kernel, out_shape=(pltpu.VMEM(query.shape, low), pltpu.VME...]
where the time goes in v5:
time: 31.7 us; the launch traced here: 31.5 us
  Pallas kernels  30.9 us (97%)
  between operations  0.64 us (2%)
    pallas_call x1, Pallas kernels, on_device(): pl.pallas_call(kernel, out_shape=(pltpu.VMEM(query.shape, low), pltpu.VME...  30 us
    pallas_call x1, Pallas kernels, on_device(): pl.pallas_call(store, out_shape=tuple((jax.ShapeDtypeStruct(a.shape, low)...  0.85 us

profile of v5, /device:TPU:231, one launch (start us, length us, event | category | flops | bytes accessed | tf_op | source)
XLA Modules:
  0.0 31.5 jit_solution(5544196921223281736)
XLA Ops:
  0.6 30.0 %shard_map.85 = (bf16[128,2048]{1,0:T(8,128)(2,1)S(1)}, bf16[2,32,1024]{2,1,0:T(8,128)(2,1)S(1)}) custom-call(bf16[128,2048]{1,0:T(8,128)(2,1)} %query.1, bf16[32,1024]{1,0:T(8,128)(2,1)} %keys.1, bf16[32,1024]{1,0:T(8,128)(2,1)} %values.1, bf16[128,2048]{1,0:T(8,128)(2,1)} %grad_out.1, f32[16,128]{1,0:T(8,128)} %bitcast.3, s32[128,128]{1,0:T(8,128)} %bitcast.2), custom_call_target="tpu_custom_call" | custom-call | tf_op jit(solution)/shard_map/pallas_call | solution.py:378
  30.6 0.9 %shard_map.86 = (bf16[128,2048]{1,0:T(8,128)(2,1)}, bf16[32,1024]{1,0:T(8,128)(2,1)}, bf16[32,1024]{1,0:T(8,128)(2,1)}) custom-call(bf16[128,2048]{1,0:T(8,128)(2,1)S(1)} %get-tuple-element.5.dq, bf16[2,32,1024]{2,1,0:T(8,128)(2,1)S(1)} %get-tuple-element.6.dkv), custom_call_target="tpu_custom_call" | custom-call | tf_op jit(solution)/shard_map/pallas_call | solution.py:413

commit v6 on v5

--- a/solution.py
+++ b/solution.py
@@ -71,9 +71,6 @@
     half = pl.ds(aligned(core, HALF), HALF)
     far_half = pl.ds(aligned(other, HALF), HALF)
     my_rows = pl.ds(aligned(core, TOK), TOK)
-    loc_stage = [local(0, keys, stage.at[0]), local(1, values, stage.at[1])]
-    loc_s = local(2, segments, sb)
-
     barrier = pltpu.get_barrier_semaphore()
     for step in STEPS:
         def greet(step=step):
@@ -86,13 +83,14 @@
 
         only_if(step, chip >= step, greet)
 
+    loc_stage = [local(0, keys, stage.at[0]), local(1, values, stage.at[1])]
+    loc_s = local(2, segments, sb)
     near = sum(jnp.where(c, 1, 0) for c in (chip + 1 < chips, chip + 2 < chips))
     pl.semaphore_wait(barrier, len(PLACES) - 1 + len(PLACES) * near)
 
     for copy in loc_stage:
         copy.wait()
     kv_copies = [[[] for _ in range(3)] for _ in range(2)]
-    loc_kv = []
 
     def send_rows(which):
         for step in STEPS:
@@ -104,7 +102,7 @@
                 cols = pl.ds(aligned(2 * ph + pcore, HD), HD)
                 kv_copies[which][step].append(remote(
                     stage.at[which, :, cols], kv.at[which, slot],
-                    kv_send.at[which, step, k], kv_recv.at[which, step, k],
+                    kv_send.at[which, step], kv_recv.at[which, step],
                     2 * (chip + step) + pcore, ph,
                 ))
 
@@ -113,7 +111,9 @@
                     copy.start()
 
             only_if(step, chip + step < chips, start)
-        loc_kv.append(local(7 + which, stage.at[which, :, mine], kv.at[which, slot]))
+        pltpu.make_async_copy(
+            stage.at[which, :, mine], kv.at[which, slot], kv_recv.at[which, 0]
+        ).start()
 
     pair_copies = []
 
@@ -191,12 +191,12 @@
 
         over_heads(body)
 
+    def settle(block, sem):
+        pltpu.make_async_copy(block, block, sem).wait()
+
     def arrival(which, step):
         def wait():
-            for copy in kv_copies[which][step]:
-                copy.wait_recv()
-            if not step:
-                loc_kv[which].wait()
+            settle(kv.at[which, pl.ds((2 - step) * PAIR, PAIR)], kv_recv.at[which, step])
 
         only_if(step, chip >= step, wait)
 
@@ -266,7 +266,6 @@
         return pl.ds(pl.multiple_of(pcore * TOK + PIECE * ph, PIECE), PIECE)
 
     back = [[[] for _ in range(3)] for _ in range(2)]
-    loc_back = [None] * 2
 
     def send_back(which, step):
         terms[which, step] = grads_of(which, 2 - step).astype(terms.dtype)
@@ -274,7 +273,7 @@
             pcore, ph = place(k)
             back[which][step].append(remote(
                 terms.at[which, step, rows_at(k)], gathered.at[which, step, :, mine],
-                back_send.at[which, step, k], back_recv.at[which, step, k],
+                back_send.at[which, step], back_recv.at[which, step],
                 2 * (chip - step) + pcore, ph,
             ))
 
@@ -285,9 +284,10 @@
         only_if(step, chip >= step, start)
         if not step:
             own_rows = rows_at(len(PLACES) - 1)
-            loc_back[which] = local(
-                9 + which, terms.at[which, 0, own_rows], gathered.at[which, 0, :, mine]
-            )
+            pltpu.make_async_copy(
+                terms.at[which, 0, own_rows], gathered.at[which, 0, :, mine],
+                back_recv.at[which, 0],
+            ).start()
 
     arrival(0, 0)
     products(0, 2)
@@ -330,29 +330,28 @@
     dq_copy.start()
     loc_dq = local(6, dqs.at[core], dq_out.at[:, half])
 
+    for copy in pair_copies:
+        copy.wait_send()
+    pieces = [pl.ds(0, PIECE * (len(PLACES) - (step == 0))) for step in range(3)]
     for which in (1, 0):
         for step in STEPS:
-            def wait(which=which, step=step):
-                for copy in back[which][step]:
-                    copy.wait_recv()
-
-            only_if(step, chip + step < chips, wait)
-        loc_back[which].wait()
+            def kv_sent():
+                settle(kv.at[which, pieces[step]], kv_send.at[which, step])
+
+            def back_sent():
+                settle(terms.at[which, step, pieces[step]], back_send.at[which, step])
+
+            def landed():
+                settle(gathered.at[which, step], back_recv.at[which, step])
+
+            only_if(step, chip + step < chips, kv_sent)
+            only_if(step, chip >= step, back_sent)
+            only_if(step, chip + step < chips, landed)
         total = gathered[which, 0].astype(jnp.float32)
         for step in (1, 2):
             total += gathered[which, step].astype(jnp.float32)
         dkv_out[which] = total.astype(dkv_out.dtype)
 
-    for copy in pair_copies:
-        copy.wait_send()
-    for which in range(2):
-        for step in STEPS:
-            def sent(copies):
-                for copy in copies:
-                    copy.wait_send()
-
-            only_if(step, chip + step < chips, lambda: sent(kv_copies[which][step]))
-            only_if(step, chip >= step, lambda: sent(back[which][step]))
     loc_dq.wait()
     dq_copy.wait()
 
@@ -374,7 +373,6 @@
     low, full = jnp.bfloat16, jnp.float32
     tokens = query.shape[0]
     dma = pltpu.SemaphoreType.DMA
-    places = len(PLACES)
     dq, dkv = pl.pallas_call(
         kernel,
         out_shape=(
@@ -401,9 +399,9 @@
             pltpu.VMEM((2, 3) + keys.shape, low),
             pltpu.VMEM((2, tokens, HALF), low),
             dma((11,)),
-            dma((2, 3, places)), dma((2, 3, places)),
+            dma((2, 3)), dma((2, 3)),
             dma((3,)), dma((3,)),
-            dma((2, 3, places)), dma((2, 3, places)),
+            dma((2, 3)), dma((2, 3)),
             dma((1,)), dma((1,)),
         ],
         compiler_params=pltpu.CompilerParams(

time: 31.7 us -> 30 us (0.946)
  Pallas kernels: 30.9 us -> 29.2 us
    pallas_call x1, Pallas kernels: 30 us -> 28.3 us  [on_device(): pl.pallas_call(kernel, out_shape=(pltpu.VMEM(query.shape, low), pltpu.VME...]
where the time goes in v6:
time: 30 us; the launch traced here: 29.8 us
  Pallas kernels  29.2 us (97%)
  between operations  0.64 us (2%)
    pallas_call x1, Pallas kernels, on_device(): pl.pallas_call(kernel, out_shape=(pltpu.VMEM(query.shape, low), pltpu.VME...  28.3 us
    pallas_call x1, Pallas kernels, on_device(): pl.pallas_call(store, out_shape=tuple((jax.ShapeDtypeStruct(a.shape, low)...  0.85 us

profile of v6, /device:TPU:231, one launch (start us, length us, event | category | flops | bytes accessed | tf_op | source)
XLA Modules:
  0.0 29.8 jit_solution(3880656323949206639)
XLA Ops:
  0.6 28.3 %shard_map.85 = (bf16[128,2048]{1,0:T(8,128)(2,1)S(1)}, bf16[2,32,1024]{2,1,0:T(8,128)(2,1)S(1)}) custom-call(bf16[128,2048]{1,0:T(8,128)(2,1)} %query.1, bf16[32,1024]{1,0:T(8,128)(2,1)} %keys.1, bf16[32,1024]{1,0:T(8,128)(2,1)} %values.1, bf16[128,2048]{1,0:T(8,128)(2,1)} %grad_out.1, f32[16,128]{1,0:T(8,128)} %bitcast.3, s32[128,128]{1,0:T(8,128)} %bitcast.2), custom_call_target="tpu_custom_call" | custom-call | tf_op jit(solution)/shard_map/pallas_call | solution.py:376
  28.9 0.9 %shard_map.86 = (bf16[128,2048]{1,0:T(8,128)(2,1)}, bf16[32,1024]{1,0:T(8,128)(2,1)}, bf16[32,1024]{1,0:T(8,128)(2,1)}) custom-call(bf16[128,2048]{1,0:T(8,128)(2,1)S(1)} %get-tuple-element.5.dq, bf16[2,32,1024]{2,1,0:T(8,128)(2,1)S(1)} %get-tuple-element.6.dkv), custom_call_target="tpu_custom_call" | custom-call | tf_op jit(solution)/shard_map/pallas_call | solution.py:411

commit v7 on v6

--- a/solution.py
+++ b/solution.py
@@ -93,7 +93,7 @@
     kv_copies = [[[] for _ in range(3)] for _ in range(2)]
 
     def send_rows(which):
-        for step in STEPS:
+        for step in (1, 2, 0):
             slot = pl.ds(
                 pl.multiple_of((4 - 2 * step + core) * TOK + PIECE * hd, PIECE), PIECE
             )

time: 30 us -> 29.1 us (0.970)
  Pallas kernels: 29.2 us -> 28.2 us
    pallas_call x1, Pallas kernels: 28.3 us -> 27.4 us  [on_device(): pl.pallas_call(kernel, out_shape=(pltpu.VMEM(query.shape, low), pltpu.VME...]
where the time goes in v7:
time: 29.1 us; the launch traced here: 28.9 us
  Pallas kernels  28.2 us (97%)
  between operations  0.64 us (2%)
    pallas_call x1, Pallas kernels, on_device(): pl.pallas_call(kernel, out_shape=(pltpu.VMEM(query.shape, low), pltpu.VME...  27.4 us
    pallas_call x1, Pallas kernels, on_device(): pl.pallas_call(store, out_shape=tuple((jax.ShapeDtypeStruct(a.shape, low)...  0.85 us

profile of v7, /device:TPU:231, one launch (start us, length us, event | category | flops | bytes accessed | tf_op | source)
XLA Modules:
  0.0 28.9 jit_solution(9178971086029574640)
XLA Ops:
  0.6 27.4 %shard_map.85 = (bf16[128,2048]{1,0:T(8,128)(2,1)S(1)}, bf16[2,32,1024]{2,1,0:T(8,128)(2,1)S(1)}) custom-call(bf16[128,2048]{1,0:T(8,128)(2,1)} %query.1, bf16[32,1024]{1,0:T(8,128)(2,1)} %keys.1, bf16[32,1024]{1,0:T(8,128)(2,1)} %values.1, bf16[128,2048]{1,0:T(8,128)(2,1)} %grad_out.1, f32[16,128]{1,0:T(8,128)} %bitcast.3, s32[128,128]{1,0:T(8,128)} %bitcast.2), custom_call_target="tpu_custom_call" | custom-call | tf_op jit(solution)/shard_map/pallas_call | solution.py:376
  28.0 0.9 %shard_map.86 = (bf16[128,2048]{1,0:T(8,128)(2,1)}, bf16[32,1024]{1,0:T(8,128)(2,1)}, bf16[32,1024]{1,0:T(8,128)(2,1)}) custom-call(bf16[128,2048]{1,0:T(8,128)(2,1)S(1)} %get-tuple-element.5.dq, bf16[2,32,1024]{2,1,0:T(8,128)(2,1)S(1)} %get-tuple-element.6.dkv), custom_call_target="tpu_custom_call" | custom-call | tf_op jit(solution)/shard_map/pallas_call | solution.py:411
